TPU v7x, 32 devices: a whole 2x2x4 slice. The times are simulated.
32 devices in a mesh: groups: 2 (over x), pair: 16 (over z, y, core).
Axes of the slice: x: 2, y: 2, z: 4, core: 2. Of those that a mesh axis runs over, the one named last changes fastest.
Arguments:
- answer_states: bfloat16 [128, 128, 5120], P(('groups', 'pair')), parts along dimension 0, may hold values from -6 to 6
- prompt_states: bfloat16 [512, 8, 5120], P(('groups', 'pair')), parts along dimension 0, may hold values from -6 to 6
- queries: bfloat16 [512, 8, 4096], P(('groups', 'pair')), parts along dimension 0, may hold values from -6 to 6
- w_key: bfloat16 [5120, 512], P('pair'), may hold values from -0.078125 to 0.078125
- w_value: bfloat16 [5120, 512], P('pair'), may hold values from -0.078125 to 0.078125
- key_gain: float32 [128], replicated, may hold values from 0.5 to 2
- query_gain: float32 [128], replicated, may hold values from 0.5 to 2
- pair_list: int32 [512, 2], P('groups'), parts along dimension 0, may hold values from 0 to 63, as said below
- answer_row: int32 [128], P('groups'), parts along dimension 0, may hold values from 0 to 63, as said below
- lengths: int32 [128], P('groups'), parts along dimension 0, may hold values from 1 to 128, 2048 in all
Outputs:
- attended: bfloat16 [512, 8, 4096], P(('groups', 'pair')), parts along dimension 0
There are 2 independent parts, one for each index of `groups`. A program takes and returns all parts, laid end to end along the dimension named above; an argument that names none is the same for every part. Nothing has to cross between parts.
Inputs may be any that keep to these rules, and one draw needn't show every extreme that they name: `pair_list`: the two ids of a row differ. Row r + 128 is row r reversed, for r < 128. The 32 ids in the rows of one device (aligned blocks of 16 rows) are distinct, and at most 2 of them have answer_row // 4 equal to one value; exactly 2 for some. `answer_row`: A permutation.
All inputs are finite; a program needn't handle non-finite values.
Results may differ from a plain program's by a relative error of at most 0.0086.
Values may be sent and summed in bfloat16 or wider, within the bound.
A program may use at most 128 MiB of HBM per device.

v0:
```python
import jax
import jax.numpy as jnp
from jax import lax
from jax.sharding import PartitionSpec as P

norm_eps = 1e-06


def head_norm(values_in, gain, heads):
    shaped = values_in.reshape(values_in.shape[:-1] + (heads, gain.shape[0]))
    scale = lax.rsqrt(jnp.mean(shaped * shaped, axis=-1, keepdims=True) + norm_eps)
    return (shaped * scale * gain).reshape(values_in.shape)


def table_lookup(table, indices):
    match = indices[..., None] == jnp.arange(table.shape[0], dtype=jnp.int32)
    return jnp.sum(jnp.where(match, table, 0), axis=-1)


def earlier_same(owners):
    width_refs = owners.shape[-1]
    earlier = jnp.arange(width_refs)[:, None] > jnp.arange(width_refs)[None, :]
    same = owners[..., :, None] == owners[..., None, :]
    return jnp.sum(same & earlier, axis=-1)


def group_partial(query_rows, key_rows, value_rows, valid, kv_heads, head_dim):
    rows_count, prompt_len, width = query_rows.shape
    key_len = key_rows.shape[1]
    groups = width // (kv_heads * head_dim)
    query_five = query_rows.reshape(rows_count, prompt_len, kv_heads, groups, head_dim)
    key_four = key_rows.reshape(rows_count, key_len, kv_heads, head_dim)
    value_four = value_rows.reshape(rows_count, key_len, kv_heads, head_dim)
    scores = jnp.einsum(
        "rqkgd,rlkd->rkgql", query_five, key_four, preferred_element_type=jnp.float32
    ) * head_dim ** (-0.5)
    weights = jnp.where(valid[:, None, None], jnp.exp(scores), 0.0)
    totals = jnp.sum(weights, axis=-1)
    numer = jnp.einsum(
        "rkgql,rlkd->rqkgd",
        weights.astype(jnp.bfloat16),
        value_four,
        preferred_element_type=jnp.float32,
    )
    totals_q = jnp.transpose(totals, (0, 3, 1, 2))
    mixed = (numer / totals_q[..., None]).astype(jnp.bfloat16)
    return (
        mixed.reshape(rows_count, prompt_len, width),
        totals_q.reshape(rows_count, prompt_len, kv_heads * groups),
    )


def per_device(
    answer_states,
    prompt_states,
    queries,
    w_key,
    w_value,
    key_gain,
    query_gain,
    pair_list,
    answer_row,
    lengths,
):
    device = lax.axis_index("pair")
    peers = lax.axis_size("pair")
    ans_dev, ans_len, width = answer_states.shape
    pairs_dev, prompt_len = (queries.shape[0], queries.shape[1])
    head_dim = key_gain.shape[0]
    kv_width = w_key.shape[1]
    kv_heads = kv_width // head_dim
    q_heads = queries.shape[2] // head_dim
    refs = 2 * pairs_dev
    capacity = (refs + peers - 1) // peers
    answer_flat = answer_states.reshape(ans_dev * ans_len, width)
    prompt_flat = prompt_states.reshape(pairs_dev * prompt_len, width)
    key_piece = lax.all_gather(w_key, "pair", axis=0, tiled=True)
    value_piece = lax.all_gather(w_value, "pair", axis=0, tiled=True)
    answer_kraw = jnp.dot(answer_flat, key_piece, preferred_element_type=jnp.float32)
    answer_vraw = jnp.dot(answer_flat, value_piece, preferred_element_type=jnp.float32)
    prompt_kraw = jnp.dot(prompt_flat, key_piece, preferred_element_type=jnp.float32)
    prompt_vraw = jnp.dot(prompt_flat, value_piece, preferred_element_type=jnp.float32)
    answer_keys = (
        head_norm(answer_kraw, key_gain, kv_heads)
        .astype(jnp.bfloat16)
        .reshape(ans_dev, ans_len, kv_width)
    )
    answer_values = answer_vraw.astype(jnp.bfloat16).reshape(ans_dev, ans_len, kv_width)
    prompt_keys = (
        head_norm(prompt_kraw, key_gain, kv_heads)
        .astype(jnp.bfloat16)
        .reshape(pairs_dev, prompt_len, kv_width)
    )
    prompt_values = prompt_vraw.astype(jnp.bfloat16).reshape(pairs_dev, prompt_len, kv_width)
    query_normed = head_norm(queries.astype(jnp.float32), query_gain, q_heads).astype(jnp.bfloat16)
    all_ids = pair_list.reshape(peers, refs)
    all_rows = table_lookup(answer_row, all_ids)
    all_owner = all_rows // ans_dev
    all_local = all_rows % ans_dev
    all_rank = earlier_same(all_owner)
    all_lens = table_lookup(lengths, all_ids)
    my_owner = lax.dynamic_index_in_dim(all_owner, device, 0, keepdims=False)
    my_rank = lax.dynamic_index_in_dim(all_rank, device, 0, keepdims=False)
    my_lens = lax.dynamic_index_in_dim(all_lens, device, 0, keepdims=False)
    fetch_index = my_owner * capacity + my_rank
    slot_range = jnp.arange(capacity, dtype=jnp.int32)
    slot_match = (all_owner == device)[:, None, :] & (
        all_rank[:, None, :] == slot_range[None, :, None]
    )
    slot_filled = jnp.any(slot_match, axis=-1)
    slot_local = jnp.sum(jnp.where(slot_match, all_local[:, None, :], 0), axis=-1)
    query_refs = jnp.repeat(query_normed, 2, axis=0)
    positions = jnp.arange(ans_len, dtype=jnp.int32)
    stacked = jnp.concatenate([answer_keys, answer_values], axis=-1)
    chosen = (slot_local[..., None] == jnp.arange(ans_dev, dtype=jnp.int32)) & slot_filled[
        ..., None
    ]
    outgoing = jnp.dot(
        chosen.reshape(peers * capacity, ans_dev).astype(jnp.bfloat16),
        stacked.reshape(ans_dev, -1),
        preferred_element_type=jnp.float32,
    )
    outgoing = outgoing.astype(jnp.bfloat16).reshape(peers, capacity, ans_len, 2 * kv_width)
    incoming = lax.all_to_all(outgoing, "pair", split_axis=0, concat_axis=0, tiled=True)
    fetched = jnp.take(
        incoming.reshape(peers * capacity, ans_len, 2 * kv_width), fetch_index, axis=0
    )
    ref_valid = jnp.broadcast_to(
        positions[None, None, :] < my_lens[:, None, None], (refs, prompt_len, ans_len)
    )
    answer_mixed, answer_totals = group_partial(
        query_refs, fetched[..., :kv_width], fetched[..., kv_width:], ref_valid, kv_heads, head_dim
    )
    causal = jnp.arange(prompt_len)[:, None] >= jnp.arange(prompt_len)[None, :]
    prompt_valid = jnp.broadcast_to(causal, (pairs_dev, prompt_len, prompt_len))
    prompt_mixed, prompt_totals = group_partial(
        query_normed, prompt_keys, prompt_values, prompt_valid, kv_heads, head_dim
    )
    side_mixed = answer_mixed.reshape(pairs_dev, 2, prompt_len, q_heads, head_dim).astype(
        jnp.float32
    )
    side_totals = answer_totals.reshape(pairs_dev, 2, prompt_len, q_heads)
    own_mixed = prompt_mixed.reshape(pairs_dev, prompt_len, q_heads, head_dim).astype(jnp.float32)
    numer = (
        jnp.sum(side_totals[..., None] * side_mixed, axis=1) + prompt_totals[..., None] * own_mixed
    )
    denom = jnp.sum(side_totals, axis=1) + prompt_totals
    return (
        (numer / denom[..., None])
        .reshape(pairs_dev, prompt_len, q_heads * head_dim)
        .astype(jnp.bfloat16)
    )


def solution(mesh):
    in_specs = (
        P(("groups", "pair"), None, None),
        P(("groups", "pair"), None, None),
        P(("groups", "pair"), None, None),
        P("pair", None),
        P("pair", None),
        P(),
        P(),
        P("groups", None),
        P("groups"),
        P("groups"),
    )
    out_specs = P(("groups", "pair"), None, None)
    return jax.shard_map(
        per_device, mesh=mesh, in_specs=in_specs, out_specs=out_specs, check_vma=False
    )
```

profile of v0, /device:TPU:13, one launch (start us, length us, event | category | flops | bytes accessed | tf_op | source)
XLA Modules:
  0.0 394.5 jit_solution(15574318022006492619)
XLA Ops:
  6.5 0.0 copy-start
  6.5 0.0 all-gather.3.cloned.1.call-start
  6.5 0.7 all-gather.3.cloned.1.call-update
  7.3 0.0 all-gather.5.cloned.1.call-start
  7.3 0.7 all-gather.5.cloned.1.call-update
  8.0 0.8 copy.114
  8.8 0.1 eq.76
  9.0 1.4 select_reduce_fusion.1
  10.4 0.5 convert_reduce_fusion
  10.9 0.1 select_reduce_fusion.2
  11.0 0.1 copy.115
  11.1 0.1 eq.88
  11.2 0.1 fusion.32
  11.3 0.1 copy.116
  11.4 0.1 and.81
  11.5 54.8 %all-gather.3.cloned.1.call-done = bf16[5120,512]{1,0:T(8,128)(2,1)} async-done(((bf16[320,512]{1,0:T(8,128)(2,1)}), bf16[5120,512]{1,0:T(8,128)(2,1)}) %all-gather.3.cloned.1.call-update) | async-done | bytes 5242896 | tf_op jit(solution)/shard_map/all_gather | solution.py:77
  66.3 8.0 %copy.117 = bf16[512,5120]{1,0:T(8,128)(2,1)} copy(bf16[512,5120]{0,1:T(8,128)(2,1)} %bitcast.129) | data formatting | bytes 10485760 | tf_op jit(solution)/shard_map/dot_general | solution.py:79
  74.3 6.8 %multiply_reduce_fusion = (f32[512,4]{0,1:T(4,128)S(1)}, f32[512,4,128]{0,2,1:T(8,128)S(1)}) fusion(bf16[512,5120,1]{1,0,2:T(8,128)(2,1)} %bitcast.142, bf16[4,128,5120]{2,1,0:T(8,128)(2,1)} %bitcast.126), kind=kOutput, calls=%fused_computation.38 | convolution fusion | flops 2684876800 | bytes 11542528 | tf_op jit(solution)/shard_map/dot_general | solution.py:79
  81.2 0.0 copy-done.4
  81.2 0.1 multiply_convert_fusion
  81.3 0.1 convert_element_type.63
  81.5 0.3 copy.118
  81.8 41.4 %all-gather.5.cloned.1.call-done = bf16[5120,512]{1,0:T(8,128)(2,1)} async-done(((bf16[320,512]{1,0:T(8,128)(2,1)}), bf16[5120,512]{1,0:T(8,128)(2,1)}) %all-gather.5.cloned.1.call-update) | async-done | bytes 5242896 | tf_op jit(solution)/shard_map/all_gather | solution.py:78
  123.2 6.9 %convolution_convert_fusion.1 = bf16[512,512]{1,0:T(8,128)(2,1)S(1)} fusion(bf16[512,5120]{1,0:T(8,128)(2,1)} %bitcast.143, bf16[5120,512]{1,0:T(8,128)(2,1)} %all-gather.5.cloned.1.call-done), kind=kOutput, calls=%fused_computation.30 | convolution fusion | flops 2684616704 | bytes 11010048 | tf_op jit(solution)/shard_map/dot_general | solution.py:80
  130.1 0.1 maximum_bitcast_fusion
  130.2 0.8 copy.153
  131.1 5.6 %convolution_convert_fusion = bf16[32,131072]{1,0:T(8,128)(2,1)} fusion(bf16[4,131072]{1,0:T(4,128)(2,1)S(1)} %bitcast.132, s32[32]{0:T(128)S(1)} %eq.88, pred[32]{0:T(512)(128)(4,1)S(1)} %and.81), kind=kOutput, calls=%fused_computation.1 | convolution fusion | flops 37748992 | bytes 9437344 | tf_op jit(solution)/shard_map/dot_general | solution.py:118
  136.7 11.3 %copy.154 = bf16[4,8,128,1024]{3,2,1,0:T(8,128)(2,1)} copy(bf16[4,8,128,1024]{3,1,2,0:T(8,128)(2,1)} %bitcast.125) | data formatting | bytes 16777216
  148.0 6.1 %all-to-all-start = ((bf16[16,2,128,1024]{3,2,1,0:T(8,128)(2,1)}), bf16[16,2,128,1024]{3,2,1,0:T(8,128)(2,1)}, u32[]{:S(2)}, u32[]{:S(2)}) async-start(bf16[16,2,128,1024]{3,2,1,0:T(8,128)(2,1)} %bitcast.124), calls=%async_computation | async-start | bytes 16777216 | tf_op jit(solution)/shard_map/all_to_all | solution.py:124
  154.2 0.0 copy-done.2
  154.2 0.6 fusion.3
  154.8 0.1 iota_compare_fusion.4
  154.9 0.0 copy-done.5
  155.0 0.7 fusion.5
  155.7 0.0 copy-done
  155.7 4.5 %multiply_reduce_fusion.1 = (f32[128,4]{0,1:T(4,128)S(1)}, f32[128,4,128]{2,0,1:T(8,128)S(1)}) fusion(bf16[4,128,5120]{2,1,0:T(8,128)(2,1)} %bitcast.127, bf16[16,8,5120]{2,1,0:T(8,128)(2,1)S(1)} %copy-done), kind=kOutput, calls=%fused_computation.42 | convolution fusion | flops 671219200 | bytes 6817792 | tf_op jit(solution)/shard_map/dot_general | solution.py:81
  160.2 6.1 %fusion.23 = f32[16,4,8,8,8]{4,2,3,1,0:T(8,128)} fusion(bf16[16,8,4,8,128]{4,1,3,2,0:T(8,128)(2,1)S(1)} %bitcast.128, f32[128,4,128]{2,0,1:T(8,128)S(1)} %get-tuple-element.18, f32[128]{0:T(128)S(1)} %copy-done.4, f32[128,4]{0,1:T(4,128)S(1)} %add_rsqrt_fusion.2), kind=kOutput, calls=%fused_computation.35 | convolution fusion | flops 8585216 | bytes 1444352 | tf_op jit(solution)/shard_map/rqkgd,rlkd->rkgql/dot_general | solution.py:34
  166.3 2.9 copy.130
  169.2 1.1 fusion.26
  170.3 3.6 copy.134
  174.0 0.2 copy.148
  174.2 0.1 copy.136
  174.3 5.1 %fusion.9 = bf16[16,8,4,8,128]{4,1,3,2,0:T(8,128)(2,1)} fusion(bf16[16,4,8,8,8]{4,3,2,1,0:T(8,128)(2,1)} %copy.134, f32[16,8,4,8]{1,3,2,0:T(8,128)S(1)} %copy.148, bf16[5120,512]{1,0:T(8,128)(2,1)} %all-gather.5.cloned.1.call-done, bf16[16,8,5120]{2,1,0:T(8,128)(2,1)S(1)} %copy-done), kind=kOutput, calls=%fused_computation.22 | convolution fusion | flops 680591360 | bytes 7684096 | tf_op jit(solution)/shard_map/rkgql,rlkd->rqkgd/dot_general | solution.py:39
  179.5 157.0 %all-to-all-done = bf16[16,2,128,1024]{3,2,1,0:T(8,128)(2,1)} async-done(((bf16[16,2,128,1024]{3,2,1,0:T(8,128)(2,1)}), bf16[16,2,128,1024]{3,2,1,0:T(8,128)(2,1)}, u32[]{:S(2)}, u32[]{:S(2)}) %all-to-all-start) | async-done | bytes 8388640 | tf_op jit(solution)/shard_map/all_to_all | solution.py:124
  336.5 8.4 %gather_fusion = bf16[32,128,1024]{2,1,0:T(8,128)(2,1)} fusion(bf16[32,128,1024]{2,1,0:T(8,128)(2,1)} %bitcast.7, s32[1024]{0:T(1024)S(1)} %pad_clamp_fusion), kind=kCustom, calls=%fused_computation | custom fusion | bytes 16777344 | tf_op jit(solution)/shard_map/jit(_take)/gather | solution.py:125
  344.9 7.5 %broadcast_select_fusion = bf16[32,128,1024]{2,1,0:T(8,128)(2,1)} fusion(bf16[32,128,1024]{2,1,0:T(8,128)(2,1)} %gather_fusion, pred[32]{0:T(512)(128)(4,1)S(1)} %get-tuple-element.7), kind=kLoop, calls=%fused_computation.2 | loop fusion | flops 4194304 | bytes 16777248 | tf_op jit(solution)/shard_map/jit(_take)/select_n | solution.py:125
  352.4 5.8 %fusion.44 = (bf16[32,128,512]{2,1,0:T(8,128)(2,1)}, bf16[32,128,512]{2,1,0:T(8,128)(2,1)}) fusion(bf16[32,128,1024]{2,1,0:T(8,128)(2,1)} %broadcast_select_fusion), kind=kLoop, calls=%fused_computation.84 | loop fusion | bytes 16777216 | tf_op jit(solution)/shard_map/slice | solution.py:132
  358.2 6.4 %copy.119 = bf16[32,128,512]{1,2,0:T(8,128)(2,1)} copy(bf16[32,128,512]{2,1,0:T(8,128)(2,1)} %get-tuple-element.11) | data formatting | bytes 8388608 | tf_op jit(solution)/shard_map/slice | solution.py:132
  364.6 0.3 broadcast_in_dim.96
  364.9 4.8 %bitcast_convert_fusion = (bf16[32,4,8,8,128]{4,2,3,1,0:T(8,128)(2,1)}, f32[32,4,128,8,8]{2,4,3,1,0:T(8,128)S(1)}) fusion(pred[32,128]{1,0:T(8,128)(4,1)S(1)} %iota_compare_fusion.4, bf16[32,128,4,128,1]{1,3,4,2,0:T(8,128)(2,1)} %bitcast.134, bf16[32,8,32,128]{3,1,2,0:T(8,128)(2,1)S(1)} %bitcast.135), kind=kOutput, calls=%fused_computation.7 | convolution fusion | flops 271581184 | bytes 12587008 | tf_op jit(solution)/shard_map/rqkgd,rlkd->rkgql/dot_general | solution.py:34
  369.7 1.2 bitcast_reduce_fusion
  370.9 0.2 copy.127
  371.1 0.1 copy.122
  371.2 6.4 %copy.124 = bf16[32,128,512]{1,2,0:T(8,128)(2,1)} copy(bf16[32,128,512]{2,1,0:T(8,128)(2,1)} %get-tuple-element.12) | data formatting | bytes 8388608 | tf_op jit(solution)/shard_map/slice | solution.py:132
  377.6 0.3 mul.140
  377.9 0.2 copy.123
  378.2 0.1 copy.137
  378.3 5.7 %fusion.1 = bf16[32,8,4,8,128]{4,1,3,2,0:T(8,128)(2,1)S(1)} fusion(bf16[32,128,4,128,1]{1,3,4,2,0:T(8,128)(2,1)} %bitcast.133, bf16[32,4,8,8,128]{4,2,3,1,0:T(8,128)(2,1)} %get-tuple-element.19, f32[32,8,4,8]{1,3,2,0:T(8,128)S(1)} %copy.127), kind=kOutput, calls=%fused_computation.6 | convolution fusion | flops 270532608 | bytes 8421376 | tf_op jit(solution)/shard_map/rkgql,rlkd->rqkgd/dot_general | solution.py:39
  384.0 0.0 copy-start.3
  384.1 0.0 copy-start.1
  384.1 1.5 fusion
  385.5 0.0 copy-done.3
  385.5 2.1 fusion.8
  387.6 0.0 copy-done.1
  (17 shorter events, 0.2 us)
Async XLA Ops:
  6.5 149.2 %copy-start = (bf16[16,8,5120]{2,1,0:T(8,128)(2,1)S(1)}, bf16[16,8,5120]{2,1,0:T(8,128)(2,1)}, u32[]{:S(2)}) copy-start(bf16[16,8,5120]{2,1,0:T(8,128)(2,1)} %param.11) | copy-start | bytes 3932164
  6.5 59.8 %all-gather.3.cloned.1.call-start = ((), (), s32[]{:S(2)}) async-start(), calls=%async_computation.1 | async-start | bytes 5570560 | tf_op jit(solution)/shard_map/all_gather | solution.py:77
  7.3 115.9 %all-gather.5.cloned.1.call-start = ((), (), s32[]{:S(2)}) async-start(), calls=%async_computation.2 | async-start | bytes 5570560 | tf_op jit(solution)/shard_map/all_gather | solution.py:78
  74.3 6.8 %copy-start.4 = (f32[128]{0:T(128)S(1)}, f32[128]{0:T(128)}, u32[]{:S(2)}) copy-start(f32[128]{0:T(128)} %param.15) | copy-start | bytes 1540
  148.0 6.2 %copy-start.2 = (bf16[16,8,4096]{2,1,0:T(8,128)(2,1)S(1)}, bf16[16,8,4096]{2,1,0:T(8,128)(2,1)}, u32[]{:S(2)}) copy-start(bf16[16,8,4096]{2,1,0:T(8,128)(2,1)} %param.12) | copy-start | bytes 3145732
  148.0 6.9 %copy-start.5 = (f32[128]{0:T(128)S(1)}, f32[128]{0:T(128)}, u32[]{:S(2)}) copy-start(f32[128]{0:T(128)} %param.16) | copy-start | bytes 1540
  148.0 188.5 %all-to-all-start = ((bf16[16,2,128,1024]{3,2,1,0:T(8,128)(2,1)}), bf16[16,2,128,1024]{3,2,1,0:T(8,128)(2,1)}, u32[]{:S(2)}, u32[]{:S(2)}) async-start(bf16[16,2,128,1024]{3,2,1,0:T(8,128)(2,1)} %bitcast.124), calls=%async_computation | async-start | bytes 16777216 | tf_op jit(solution)/shard_map/all_to_all | solution.py:124
  384.0 1.5 copy-start.3
  384.1 3.6 copy-start.1
Sparse Core Ops, SparseCore 0:
  9.6 56.6 all-gather.2
  68.6 54.5 all-gather.4
where the time goes:
time: 395 us; the launch traced here: 394 us
  waiting for transfers between devices  255 us (65%)
  local copies, waits for them, and re-layouts  57.1 us (14%)
  matrix products  45.5 us (12%)
  other arithmetic  17.2 us (4%)
  between operations  13.7 us (3%)
  starting transfers between devices  6.17 us (2%)
    all_to_all x1, waiting for transfers between devices, per_device(): lax.all_to_all(outgoing, 'pair', split_axis=0, concat_axis=0, tiled=True)  157 us
    all_gather x1, waiting for transfers between devices, per_device(): key_piece = lax.all_gather(w_key, 'pair', axis=0, tiled=True)  54.8 us
    all_gather x1, waiting for transfers between devices, per_device(): value_piece = lax.all_gather(w_value, 'pair', axis=0, tiled=True)  41.4 us
    unnamed x15, local copies, waits for them, and re-layouts  13 us
    slice x2, local copies, waits for them, and re-layouts, per_device(): fetched[..., :kv_width]  12.2 us
    dot_general x2, matrix products, group_partial(): jnp.einsum('rqkgd,rlkd->rkgql', query_five, key_four, preferred_element_t...  10.9 us
    dot_general x2, matrix products, group_partial(): jnp.einsum('rkgql,rlkd->rqkgd', weights.astype(jnp.bfloat16), value_four,...  10.9 us
    gather x1, local copies, waits for them, and re-layouts, per_device(): jnp.take(incoming.reshape(peers * capacity, ans_len, 2 * kv_width), fetch...  8.38 us
  transfers between devices with their start and end apart: 3, of which 3 were waited for; matrix products, arithmetic and copies ran while one was open for 11% of the time, Pallas kernels for 0%

commit v1 on v0

v1 whole, which is shorter than its diff:
```python
import functools
import jax
import jax.numpy as jnp
from jax import lax
from jax.experimental import pallas as pl
from jax.experimental.pallas import tpu as pltpu
from jax.sharding import PartitionSpec as P

norm_eps = 1e-06
VMEM = pltpu.VMEM
LIMIT = 48 * 1024 * 1024
USE_RING = False


def table_lookup(table, indices):
    match = indices[..., None] == jnp.arange(table.shape[0], dtype=jnp.int32)
    return jnp.sum(jnp.where(match, table, 0), axis=-1)


def earlier_same(owners):
    width_refs = owners.shape[-1]
    earlier = jnp.arange(width_refs)[:, None] > jnp.arange(width_refs)[None, :]
    same = owners[..., :, None] == owners[..., None, :]
    return jnp.sum(same & earlier, axis=-1)


def norm_rows(x, gain):
    scale = lax.rsqrt(jnp.mean(x * x, axis=-1, keepdims=True) + norm_eps)
    return x * scale * gain


def query_kernel(pairs, plen, heads, hd, slots, idx_ref, q_ref, gain_ref, own_ref, out_ref):
    gain = gain_ref[...]
    for two in range(heads // 2):
        parts = [
            norm_rows(q_ref[:, (2 * two + e) * hd : (2 * two + e + 1) * hd].astype(jnp.float32), gain)
            for e in range(2)
        ]
        for p in range(pairs):
            rows = jnp.concatenate([x[p * plen : (p + 1) * plen] for x in parts], axis=0)
            own_ref[p, two * 2 * plen : (two + 1) * 2 * plen, :] = rows.astype(jnp.bfloat16)

    def body(s, carry):
        out_ref[s] = own_ref[idx_ref[s]]
        return carry

    lax.fori_loop(0, slots, body, 0)


def prepare_queries(idx, queries, gain):
    pairs, plen, width = queries.shape
    hd = gain.shape[0]
    heads = width // hd
    slots = idx.shape[0]
    return pl.pallas_call(
        functools.partial(query_kernel, pairs, plen, heads, hd, slots),
        out_shape=[
            jax.ShapeDtypeStruct((pairs, heads * plen, hd), jnp.bfloat16),
            jax.ShapeDtypeStruct((slots, heads * plen, hd), jnp.bfloat16),
        ],
        in_specs=[
            pl.BlockSpec(memory_space=pltpu.SMEM),
            pl.BlockSpec(memory_space=VMEM),
            pl.BlockSpec(memory_space=VMEM),
        ],
        out_specs=[pl.BlockSpec(memory_space=VMEM)] * 2,
        compiler_params=pltpu.CompilerParams(vmem_limit_bytes=LIMIT),
    )(idx, queries.reshape(pairs * plen, width), gain.reshape(1, hd))


def project_kernel(hd, x_ref, wk_ref, wv_ref, gain_ref, k_ref, v_ref):
    x = x_ref[...]
    raw = jnp.dot(x, wk_ref[...], preferred_element_type=jnp.float32)
    for h in range(raw.shape[1] // hd):
        cols = slice(h * hd, (h + 1) * hd)
        k_ref[:, cols] = norm_rows(raw[:, cols], gain_ref[...]).astype(jnp.bfloat16)
    v_ref[...] = jnp.dot(x, wv_ref[...], preferred_element_type=jnp.float32).astype(jnp.bfloat16)


def project(x, wk, wv, gain):
    rows, width = x.shape
    kvw = wk.shape[1]
    hd = gain.shape[0]
    block = 128
    whole = pl.BlockSpec((width, kvw), lambda i: (0, 0), pipeline_mode=pl.Buffered(1))
    return pl.pallas_call(
        functools.partial(project_kernel, hd),
        grid=(rows // block,),
        out_shape=[jax.ShapeDtypeStruct((rows, kvw), jnp.bfloat16)] * 2,
        in_specs=[
            pl.BlockSpec((block, width), lambda i: (i, 0)),
            whole,
            whole,
            pl.BlockSpec((1, hd), lambda i: (0, 0)),
        ],
        out_specs=[pl.BlockSpec((block, kvw), lambda i: (i, 0))] * 2,
        compiler_params=pltpu.CompilerParams(vmem_limit_bytes=LIMIT),
    )(x, wk, wv, gain.reshape(1, hd))


def attend(q, k, v, valid, scale):
    scores = lax.dot_general(q, k, (((1,), (1,)), ((), ())), preferred_element_type=jnp.float32) * scale
    weights = jnp.where(valid, jnp.exp(scores), 0.0)
    total = jnp.sum(weights, axis=-1, keepdims=True)
    numer = jnp.dot(weights.astype(jnp.bfloat16), v, preferred_element_type=jnp.float32)
    return (numer / total).astype(jnp.bfloat16), total


def owner_kernel(per, kvh, hd, scale, slot_ref, len_ref, q_ref, k_ref, v_ref, o_ref, t_ref):
    step = pl.program_id(0)
    rows = q_ref.shape[1]
    each = rows // kvh
    for e in range(per):
        ref = step * per + e
        row = slot_ref[ref]
        count = len_ref[ref]
        totals = []
        for h in range(kvh):
            cols = slice(h * hd, (h + 1) * hd)
            keys = k_ref[row, :, cols]
            position = lax.broadcasted_iota(jnp.int32, (each, keys.shape[0]), 1)
            mixed, total = attend(
                q_ref[e, h * each : (h + 1) * each, :], keys, v_ref[row, :, cols], position < count, scale
            )
            o_ref[e, h * each : (h + 1) * each, :] = mixed
            totals.append(jnp.broadcast_to(total, (each, hd)))
        t_ref[e] = jnp.concatenate(totals, axis=0).T[:8]


def owner_attention(slot, lens, q, keys, values, hd):
    slots, rows, _ = q.shape
    _, alen, kvw = keys.shape
    per = 4
    spec = lambda shape, f: pl.BlockSpec(shape, f)
    return pl.pallas_call(
        functools.partial(owner_kernel, per, kvw // hd, hd, hd ** (-0.5)),
        grid_spec=pltpu.PrefetchScalarGridSpec(
            num_scalar_prefetch=2,
            grid=(slots // per,),
            in_specs=[
                spec((per, rows, hd), lambda i, *_: (i, 0, 0)),
                spec(keys.shape, lambda i, *_: (0, 0, 0)),
                spec(keys.shape, lambda i, *_: (0, 0, 0)),
            ],
            out_specs=[
                spec((per, rows, hd), lambda i, *_: (i, 0, 0)),
                spec((per, 8, rows), lambda i, *_: (i, 0, 0)),
            ],
        ),
        out_shape=[
            jax.ShapeDtypeStruct((slots, rows, hd), jnp.bfloat16),
            jax.ShapeDtypeStruct((slots, 8, rows), jnp.float32),
        ],
        compiler_params=pltpu.CompilerParams(vmem_limit_bytes=LIMIT),
    )(slot, lens, q, keys, values)


def combine_kernel(per, plen, kvh, hd, scale, at_ref, q_ref, k_ref, v_ref, in_ref, t_ref, o_ref):
    step = pl.program_id(0)
    rows = q_ref.shape[1]
    each = rows // kvh
    keys_count = k_ref.shape[0]
    results = []
    for e in range(per):
        pair = step * per + e
        place = lax.broadcasted_iota(jnp.int32, (each, keys_count), 1)
        token = lax.broadcasted_iota(jnp.int32, (each, keys_count), 0) % plen
        valid = (place // plen == pair) & (place % plen <= token)
        numers, denoms = [], []
        for h in range(kvh):
            cols = slice(h * hd, (h + 1) * hd)
            mixed, total = attend(
                q_ref[e, h * each : (h + 1) * each, :], k_ref[:, cols], v_ref[:, cols], valid, scale
            )
            numers.append(total * mixed.astype(jnp.float32))
            denoms.append(jnp.broadcast_to(total, (each, hd)))
        numer = jnp.concatenate(numers, axis=0)
        denom = jnp.concatenate(denoms, axis=0)
        for side in range(2):
            at = at_ref[pair * 2 + side]
            total = jnp.broadcast_to(t_ref[at][:1], (hd, rows)).T
            numer = numer + total * in_ref[at].astype(jnp.float32)
            denom = denom + total
        results.append(numer / denom)
    for head in range(rows // plen):
        block = jnp.concatenate([r[head * plen : (head + 1) * plen] for r in results], axis=0)
        o_ref[:, head * hd : (head + 1) * hd] = block.astype(jnp.bfloat16)


def combine(at, q, keys, values, incoming, totals, plen, hd):
    pairs, rows, _ = q.shape
    slots = incoming.shape[0]
    kvw = keys.shape[1]
    per = 4
    heads = rows // plen
    return pl.pallas_call(
        functools.partial(combine_kernel, per, plen, kvw // hd, hd, hd ** (-0.5)),
        grid_spec=pltpu.PrefetchScalarGridSpec(
            num_scalar_prefetch=1,
            grid=(pairs // per,),
            in_specs=[
                pl.BlockSpec((per, rows, hd), lambda i, *_: (i, 0, 0)),
                pl.BlockSpec(keys.shape, lambda i, *_: (0, 0)),
                pl.BlockSpec(keys.shape, lambda i, *_: (0, 0)),
                pl.BlockSpec(incoming.shape, lambda i, *_: (0, 0, 0)),
                pl.BlockSpec(totals.shape, lambda i, *_: (0, 0, 0)),
            ],
            out_specs=pl.BlockSpec((per * plen, heads * hd), lambda i, *_: (i, 0)),
        ),
        out_shape=jax.ShapeDtypeStruct((pairs * plen, heads * hd), jnp.bfloat16),
        compiler_params=pltpu.CompilerParams(vmem_limit_bytes=LIMIT),
    )(at, q, keys, values, incoming, totals)


def ring_kernel(chips, wk_ref, wv_ref, ok_ref, ov_ref, own_sem, ring_send, ring_recv, side_send, side_recv):
    me = lax.axis_index("pair")
    group = lax.axis_index("groups")
    depth = wk_ref.shape[0]
    chip, core = me // 2, me % 2
    even = chip % 2
    position = jnp.where(even == 0, chip // 2, chips - 1 - chip // 2)

    def chip_at(place):
        place = (place + 2 * chips) % chips
        return jnp.where(place < chips // 2, 2 * place, 2 * (chips - 1 - place) + 1)

    right = chip_at(position + 1) * 2 + core
    left = chip_at(position - 1) * 2 + core
    sibling = chip * 2 + 1 - core
    partners = (right, left)
    mesh_id = pl.DeviceIdType.MESH

    barrier = pltpu.get_barrier_semaphore()
    for other in (right, left, sibling):
        pl.semaphore_signal(barrier, inc=1, device_id=(group, other), device_id_type=mesh_id)
    own = []
    outs = (ok_ref, ov_ref)
    for w, (src, out) in enumerate(((wk_ref, ok_ref), (wv_ref, ov_ref))):
        copy = pltpu.make_async_copy(src, out.at[me], own_sem.at[w])
        copy.start()
        own.append(copy)
    for copy in own:
        copy.wait()
    pl.semaphore_wait(barrier, 3)

    def piece(w, step):
        return chip_at(position - step if w == 0 else position + step) * 2 + core

    def ring(w, step):
        block = outs[w].at[piece(w, step)]
        return pltpu.make_async_remote_copy(
            src_ref=block, dst_ref=block, send_sem=ring_send.at[w, step], recv_sem=ring_recv.at[w, step],
            device_id=(group, partners[w]), device_id_type=mesh_id,
        )

    def arriving(w, step):
        block = outs[w].at[piece(w, step + 1)]
        return pltpu.make_async_remote_copy(
            src_ref=block, dst_ref=block, send_sem=ring_send.at[w, step], recv_sem=ring_recv.at[w, step],
            device_id=(group, partners[w]), device_id_type=mesh_id,
        )

    def across(w, step, mine):
        block = outs[w].at[piece(w, step) if mine else chip_at(position - step if w == 0 else position + step) * 2 + 1 - core]
        return pltpu.make_async_remote_copy(
            src_ref=block, dst_ref=block, send_sem=side_send.at[w, step], recv_sem=side_recv.at[w, step],
            device_id=(group, sibling), device_id_type=mesh_id,
        )

    for w in range(2):
        ring(w, 0).start()
        across(w, 0, True).start()

    def body(step, carry):
        for w in range(2):
            arriving(w, step - 1).wait_recv()

            @pl.when(step < chips - 1)
            def _():
                ring(w, step).start()

            across(w, step, True).start()
        return carry

    lax.fori_loop(1, chips, body, 0)

    def drain(step, carry):
        for w in range(2):
            across(w, step, True).wait_send()
            across(w, step, False).wait_recv()

            @pl.when(step < chips - 1)
            def _():
                ring(w, step).wait_send()

        return carry

    lax.fori_loop(0, chips, drain, 0)


def gather_weights(w_key, w_value):
    peers = lax.axis_size("pair")
    depth, kvw = w_key.shape
    if not USE_RING:
        return tuple(lax.all_gather(w, "pair", axis=0, tiled=True) for w in (w_key, w_value))
    chips = peers // 2
    hbm = pl.BlockSpec(memory_space=pl.ANY)
    out = pl.pallas_call(
        functools.partial(ring_kernel, chips),
        out_shape=[jax.ShapeDtypeStruct((peers, depth, kvw), jnp.bfloat16)] * 2,
        in_specs=[hbm] * 2,
        out_specs=[hbm] * 2,
        scratch_shapes=[pltpu.SemaphoreType.DMA((2,))] + [pltpu.SemaphoreType.DMA((2, chips))] * 4,
        compiler_params=pltpu.CompilerParams(
            collective_id=0, has_side_effects=True, vmem_limit_bytes=LIMIT
        ),
    )(w_key, w_value)
    return tuple(w.reshape(peers * depth, kvw) for w in out)


def per_device(
    answer_states, prompt_states, queries, w_key, w_value, key_gain, query_gain, pair_list, answer_row, lengths
):
    device = lax.axis_index("pair")
    peers = lax.axis_size("pair")
    ans_dev, ans_len, width = answer_states.shape
    pairs_dev, prompt_len = (queries.shape[0], queries.shape[1])
    head_dim = key_gain.shape[0]
    kv_width = w_key.shape[1]
    refs = 2 * pairs_dev
    capacity = (refs + peers - 1) // peers
    slots = peers * capacity

    all_ids = pair_list.reshape(peers, refs)
    all_rows = table_lookup(answer_row, all_ids)
    all_owner = all_rows // ans_dev
    all_local = all_rows % ans_dev
    all_rank = earlier_same(all_owner)
    all_lens = table_lookup(lengths, all_ids)
    my_owner = lax.dynamic_index_in_dim(all_owner, device, 0, keepdims=False)
    my_rank = lax.dynamic_index_in_dim(all_rank, device, 0, keepdims=False)
    fetch_index = my_owner * capacity + my_rank
    slot_ids = jnp.arange(slots, dtype=jnp.int32)
    ref_match = fetch_index[None, :] == slot_ids[:, None]
    ref_pair = jnp.sum(jnp.where(ref_match, jnp.arange(refs, dtype=jnp.int32)[None, :] // 2, 0), axis=1)
    slot_range = jnp.arange(capacity, dtype=jnp.int32)
    slot_match = (all_owner == device)[:, None, :] & (all_rank[:, None, :] == slot_range[None, :, None])
    slot_local = jnp.sum(jnp.where(slot_match, all_local[:, None, :], 0), axis=-1).reshape(slots)
    slot_lens = jnp.sum(jnp.where(slot_match, all_lens[:, None, :], 0), axis=-1).reshape(slots)
    slot_lens = jnp.maximum(slot_lens, 1)

    query_own, outgoing = prepare_queries(ref_pair, queries, query_gain)
    asked = lax.all_to_all(outgoing, "pair", split_axis=0, concat_axis=0, tiled=True)
    key_full, value_full = gather_weights(w_key, w_value)
    answer_keys, answer_values = project(
        answer_states.reshape(ans_dev * ans_len, width), key_full, value_full, key_gain
    )
    mixed, totals = owner_attention(
        slot_local,
        slot_lens,
        asked,
        answer_keys.reshape(ans_dev, ans_len, kv_width),
        answer_values.reshape(ans_dev, ans_len, kv_width),
        head_dim,
    )
    mixed_in = lax.all_to_all(mixed, "pair", split_axis=0, concat_axis=0, tiled=True)
    totals_in = lax.all_to_all(totals, "pair", split_axis=0, concat_axis=0, tiled=True)
    prompt_keys, prompt_values = project(
        prompt_states.reshape(pairs_dev * prompt_len, width), key_full, value_full, key_gain
    )
    out = combine(
        fetch_index, query_own, prompt_keys, prompt_values, mixed_in, totals_in, prompt_len, head_dim
    )
    return out.reshape(queries.shape)


def solution(mesh):
    in_specs = (
        P(("groups", "pair"), None, None),
        P(("groups", "pair"), None, None),
        P(("groups", "pair"), None, None),
        P("pair", None),
        P("pair", None),
        P(),
        P(),
        P("groups", None),
        P("groups"),
        P("groups"),
    )
    out_specs = P(("groups", "pair"), None, None)
    return jax.shard_map(
        per_device, mesh=mesh, in_specs=in_specs, out_specs=out_specs, check_vma=False
    )
```

time: 395 us -> 278 us (0.70)
  waiting for transfers between devices: 255 us -> 175 us
  Pallas kernels: 0 us -> 51.4 us
  local copies, waits for them, and re-layouts: 57.1 us -> 10.5 us
  matrix products: 45.5 us -> 0 us
  other arithmetic: 17.2 us -> 2.16 us
  blocking collectives: 0 us -> 12.4 us
  starting transfers between devices: 6.17 us -> 12.6 us
    all_to_all x1, waiting for transfers between devices: 157 us -> 0.01 us  [per_device(): lax.all_to_all(outgoing, 'pair', split_axis=0, concat_axis=0, tiled=True)]
    pallas_call x0 -> x5, Pallas kernels: none -> 51.4 us  [the longest x1 21.8 us: owner_attention(): pl.pallas_call(functools.partial(owner_kernel, per, kvw // hd, hd, hd **...]
    dot_general x8 -> x0, matrix products: 45.5 us -> none  [the longest x2 10.9 us: group_partial(): jnp.einsum('rqkgd,rlkd->rkgql', query_five, key_four, preferred_element_t...]
    all_to_all x0 -> x1, waiting for transfers between devices: none -> 41.2 us  [per_device(): lax.all_to_all(mixed, 'pair', split_axis=0, concat_axis=0, tiled=True)]
    all_gather x2, waiting for transfers between devices: 96.3 us -> 133 us  [gather_weights(): lax.all_gather(w, 'pair', axis=0, tiled=True)]
    slice x3 -> x0, local copies, waits for them, and re-layouts: 18.7 us -> none  [the longest x2 12.2 us: per_device(): fetched[..., :kv_width]]
    all_to_all x0 -> x1, blocking collectives: none -> 12.4 us  [per_device(): lax.all_to_all(totals, 'pair', split_axis=0, concat_axis=0, tiled=True)]
    dot_general x2 -> x0, local copies, waits for them, and re-layouts: 10.9 us -> none  [the longest x1 8.02 us: per_device(): jnp.dot(answer_flat, key_piece, preferred_element_type=jnp.float32)]
  transfers between devices with their start and end apart: 3 -> 4, of which waited for: 3 -> 3; matrix products, arithmetic and copies ran while one was open for 11% -> 1% of each run, Pallas kernels for 0% -> 6%
where the time goes in v1:
time: 278 us
  waiting for transfers between devices  175 us (63%)
  Pallas kernels  51.4 us (18%)
  between operations  13.5 us (5%)
  starting transfers between devices  12.6 us (5%)
  blocking collectives  12.4 us (4%)
  local copies, waits for them, and re-layouts  10.5 us (4%)
    all_gather x2, waiting for transfers between devices, gather_weights(): lax.all_gather(w, 'pair', axis=0, tiled=True)  133 us
    all_to_all x1, waiting for transfers between devices, per_device(): lax.all_to_all(mixed, 'pair', split_axis=0, concat_axis=0, tiled=True)  41.2 us
    pallas_call x1, Pallas kernels, owner_attention(): pl.pallas_call(functools.partial(owner_kernel, per, kvw // hd, hd, hd **...  21.8 us
    pallas_call x2, Pallas kernels, project(): pl.pallas_call(functools.partial(project_kernel, hd), grid=(rows // block...  16.2 us
    all_to_all x1, blocking collectives, per_device(): lax.all_to_all(totals, 'pair', split_axis=0, concat_axis=0, tiled=True)  12.4 us
    pallas_call x1, Pallas kernels, combine(): pl.pallas_call(functools.partial(combine_kernel, per, plen, kvw // hd, hd...  12 us
    unnamed x23, local copies, waits for them, and re-layouts  10 us
    all_to_all x1, starting transfers between devices, per_device(): lax.all_to_all(outgoing, 'pair', split_axis=0, concat_axis=0, tiled=True)  6.69 us
  transfers between devices with their start and end apart: 4, of which 3 were waited for; matrix products, arithmetic and copies ran while one was open for 1% of the time, Pallas kernels for 6%

profile of v1, /device:TPU:13, one launch (start us, length us, event | category | flops | bytes accessed | tf_op | source)
XLA Modules:
  0.0 277.9 jit_solution(12873783924354353628)
XLA Ops:
  6.5 0.0 all-gather.3.cloned.1.call-start
  6.5 0.7 all-gather.3.cloned.1.call-update
  7.3 0.0 all-gather.5.cloned.1.call-start
  7.3 0.7 all-gather.5.cloned.1.call-update
  8.0 0.8 copy.12
  8.8 0.1 eq.34
  9.0 1.4 select_reduce_fusion
  10.4 0.5 convert_reduce_fusion
  10.9 0.1 select_reduce_fusion.4.idx_ref
  11.0 0.0 copy-start.6
  11.0 1.2 copy-done.6
  12.2 0.0 copy-start.10
  12.2 0.7 copy-done.10
  12.9 1.4 shard_map.100
  14.3 0.0 copy-start
  14.3 1.3 copy-done
  15.7 0.0 copy-start.3
  15.7 1.0 copy-done.3
  16.6 0.0 copy-start.9
  16.6 6.7 %all-to-all-start = ((bf16[32,256,128]{2,1,0:T(8,128)(2,1)}), bf16[32,256,128]{2,1,0:T(8,128)(2,1)S(1)}, u32[]{:S(2)}, u32[]{:S(2)}) async-start(bf16[32,256,128]{2,1,0:T(8,128)(2,1)} %copy-done), calls=%async_computation | async-start | bytes 4194304 | tf_op jit(solution)/shard_map/all_to_all | solution.py:353
  23.3 0.1 select_reduce_fusion.2
  23.5 0.1 copy.14
  23.6 0.1 max.7.len_ref
  23.7 0.1 copy.13
  23.7 0.1 reshape.140.slot_ref
  23.8 70.0 %all-gather.3.cloned.1.call-done.wk_ref = bf16[5120,512]{1,0:T(8,128)(2,1)} async-done(((bf16[320,512]{1,0:T(8,128)(2,1)}), bf16[5120,512]{1,0:T(8,128)(2,1)}) %all-gather.3.cloned.1.call-update) | async-done | bytes 5242896 | tf_op jit(solution)/shard_map/all_gather | solution.py:305
  93.9 62.6 %all-gather.5.cloned.1.call-done.wv_ref = bf16[5120,512]{1,0:T(8,128)(2,1)} async-done(((bf16[320,512]{1,0:T(8,128)(2,1)}), bf16[5120,512]{1,0:T(8,128)(2,1)}) %all-gather.5.cloned.1.call-update) | async-done | bytes 5242896 | tf_op jit(solution)/shard_map/all_gather | solution.py:305
  156.5 0.0 copy-done.9
  156.5 10.6 %shard_map.102 = (bf16[512,512]{1,0:T(8,128)(2,1)S(1)}, bf16[512,512]{1,0:T(8,128)(2,1)S(1)}) custom-call(bf16[512,5120]{1,0:T(8,128)(2,1)} %bitcast.17, bf16[5120,512]{1,0:T(8,128)(2,1)} %all-gather.3.cloned.1.call-done.wk_ref, bf16[5120,512]{1,0:T(8,128)(2,1)} %all-gather.5.cloned.1.call-done.wv_ref, f32[1,128]{1,0:T(1,128)S(1)} %bitcast.14), custom_call_target="tpu_custom_call" | custom-call | tf_op jit(solution)/shard_map/pallas_call | solution.py:86
  167.1 0.0 all-to-all-done.q_ref
  167.1 21.8 %shard_map.103 = (bf16[32,256,128]{2,1,0:T(8,128)(2,1)S(1)}, f32[32,8,256]{2,1,0:T(8,128)S(1)}) custom-call(s32[32]{0:T(128)S(1)} %reshape.140.slot_ref, s32[32]{0:T(128)S(1)} %max.7.len_ref, bf16[32,256,128]{2,1,0:T(8,128)(2,1)S(1)} %all-to-all-done.q_ref, bf16[4,128,512]{2,1,0:T(8,128)(2,1)S(1)} %bitcast.12, bf16[4,128,512]{2,1,0:T(8,128)(2,1)S(1)} %bitcast.13), custom_call_target="tpu_custom_call" | custom-call | tf_op jit(solution)/shard_map/pallas_call | solution.py:135
  188.9 0.0 copy-start.1
  188.9 1.3 copy-done.1
  190.3 12.4 %all_to_all.15.t_ref = f32[32,8,256]{2,1,0:T(8,128)} all-to-all(f32[32,8,256]{2,1,0:T(8,128)S(1)} %get-tuple-element.20), channel_id=1, replica_groups=mesh['groups'=2,'pair'=16] {'pair'}, dimensions={0} | all-to-all | bytes 524288 | tf_op jit(solution)/shard_map/all_to_all | solution.py:367
  202.7 0.0 copy-start.2
  202.7 5.9 %all-to-all-start.1 = ((bf16[32,256,128]{2,1,0:T(8,128)(2,1)}), bf16[32,256,128]{2,1,0:T(8,128)(2,1)S(1)}, u32[]{:S(2)}, u32[]{:S(2)}) async-start(bf16[32,256,128]{2,1,0:T(8,128)(2,1)} %copy-done.1), calls=%async_computation.1 | async-start | bytes 4194304 | tf_op jit(solution)/shard_map/all_to_all | solution.py:366
  208.5 0.0 copy-done.2
  208.6 5.6 %shard_map.101 = (bf16[128,512]{1,0:T(8,128)(2,1)S(1)}, bf16[128,512]{1,0:T(8,128)(2,1)S(1)}) custom-call(bf16[128,5120]{1,0:T(8,128)(2,1)S(1)} %bitcast.10, bf16[5120,512]{1,0:T(8,128)(2,1)} %all-gather.3.cloned.1.call-done.wk_ref, bf16[5120,512]{1,0:T(8,128)(2,1)} %all-gather.5.cloned.1.call-done.wv_ref, f32[1,128]{1,0:T(1,128)S(1)} %bitcast.15), custom_call_target="tpu_custom_call" | custom-call | tf_op jit(solution)/shard_map/pallas_call | solution.py:86
  214.1 0.0 copy-start.7
  214.1 0.6 copy-done.7
  214.8 41.2 %all-to-all-done.1.in_ref = bf16[32,256,128]{2,1,0:T(8,128)(2,1)S(1)} async-done(((bf16[32,256,128]{2,1,0:T(8,128)(2,1)}), bf16[32,256,128]{2,1,0:T(8,128)(2,1)S(1)}, u32[]{:S(2)}, u32[]{:S(2)}) %all-to-all-start.1) | async-done | bytes 2097184 | tf_op jit(solution)/shard_map/all_to_all | solution.py:366
  256.0 0.0 copy-start.4
  256.0 1.2 copy-done.4
  257.2 0.0 copy-start.5
  257.2 0.9 copy-done.5
  258.2 0.0 copy-start.8
  258.2 0.9 copy-done.8
  259.1 12.0 %shard_map.104 = bf16[128,4096]{1,0:T(8,128)(2,1)} custom-call(s32[32]{0:T(128)S(1)} %add_bitcast_fusion.at_ref, bf16[16,256,128]{2,1,0:T(8,128)(2,1)S(1)} %copy-done.4, bf16[128,512]{1,0:T(8,128)(2,1)S(1)} %get-tuple-element.14.k_ref, bf16[128,512]{1,0:T(8,128)(2,1)S(1)} %copy-done.8, bf16[32,256,128]{2,1,0:T(8,128)(2,1)S(1)} %all-to-all-done.1.in_ref, ...), custom_call_target="tpu_custom_call" | custom-call | tf_op jit(solution)/shard_map/pallas_call | solution.py:196
  (6 shorter events, 0.1 us)
Async XLA Ops:
  6.5 87.3 %all-gather.3.cloned.1.call-start = ((), (), s32[]{:S(2)}) async-start(), calls=%async_computation.3 | async-start | bytes 5570560 | tf_op jit(solution)/shard_map/all_gather | solution.py:305
  7.3 149.3 %all-gather.5.cloned.1.call-start = ((), (), s32[]{:S(2)}) async-start(), calls=%async_computation.4 | async-start | bytes 5570560 | tf_op jit(solution)/shard_map/all_gather | solution.py:305
  11.0 1.2 copy-start.6
  12.2 0.7 copy-start.10
  14.3 1.3 copy-start
  15.7 1.0 copy-start.3
  16.6 139.9 %copy-start.9 = (f32[128]{0:T(128)S(1)}, f32[128]{0:T(128)}, u32[]{:S(2)}) copy-start(f32[128]{0:T(128)} %param.15) | copy-start | bytes 1540
  16.6 150.5 %all-to-all-start = ((bf16[32,256,128]{2,1,0:T(8,128)(2,1)}), bf16[32,256,128]{2,1,0:T(8,128)(2,1)S(1)}, u32[]{:S(2)}, u32[]{:S(2)}) async-start(bf16[32,256,128]{2,1,0:T(8,128)(2,1)} %copy-done), calls=%async_computation | async-start | bytes 4194304 | tf_op jit(solution)/shard_map/all_to_all | solution.py:353
  188.9 1.3 copy-start.1
  202.7 5.9 %copy-start.2 = (bf16[16,8,5120]{2,1,0:T(8,128)(2,1)S(1)}, bf16[16,8,5120]{2,1,0:T(8,128)(2,1)}, u32[]{:S(2)}) copy-start(bf16[16,8,5120]{2,1,0:T(8,128)(2,1)} %param.11) | copy-start | bytes 3932164
  202.7 53.3 %all-to-all-start.1 = ((bf16[32,256,128]{2,1,0:T(8,128)(2,1)}), bf16[32,256,128]{2,1,0:T(8,128)(2,1)S(1)}, u32[]{:S(2)}, u32[]{:S(2)}) async-start(bf16[32,256,128]{2,1,0:T(8,128)(2,1)} %copy-done.1), calls=%async_computation.1 | async-start | bytes 4194304 | tf_op jit(solution)/shard_map/all_to_all | solution.py:366
  214.1 0.6 copy-start.7
  256.0 1.2 copy-start.4
  257.2 0.9 copy-start.5
  258.2 0.9 copy-start.8
Sparse Core Ops, SparseCore 0:
  9.6 84.1 all-gather.2
  96.2 60.3 all-gather.4

commit v2 on v1

--- a/solution.py
+++ b/solution.py
@@ -9,7 +9,7 @@
 norm_eps = 1e-06
 VMEM = pltpu.VMEM
 LIMIT = 48 * 1024 * 1024
-USE_RING = False
+USE_RING = True
 
 
 def table_lookup(table, indices):
@@ -218,11 +218,12 @@
     depth = wk_ref.shape[0]
     chip, core = me // 2, me % 2
     even = chip % 2
-    position = jnp.where(even == 0, chip // 2, chips - 1 - chip // 2)
+    position = (1 - even) * (chip // 2) + even * (chips - 1 - chip // 2)
 
     def chip_at(place):
         place = (place + 2 * chips) % chips
-        return jnp.where(place < chips // 2, 2 * place, 2 * (chips - 1 - place) + 1)
+        back = place // (chips // 2)
+        return (1 - back) * 2 * place + back * (2 * (chips - 1 - place) + 1)
 
     right = chip_at(position + 1) * 2 + core
     left = chip_at(position - 1) * 2 + core

time: 278 us -> 236 us (0.85)
  waiting for transfers between devices: 175 us -> 41.2 us
  Pallas kernels: 51.4 us -> 153 us
  between operations: 13.5 us -> 0.17 us
    all_gather x2 -> x0, waiting for transfers between devices: 133 us -> none  [gather_weights(): lax.all_gather(w, 'pair', axis=0, tiled=True)]
    pallas_call x0 -> x1, Pallas kernels: none -> 102 us  [gather_weights(): pl.pallas_call(functools.partial(ring_kernel, chips), out_shape=[jax.Shap...]
    unnamed x23 -> x29, local copies, waits for them, and re-layouts: 10 us -> 12.4 us
  transfers between devices with their start and end apart: 4 -> 2, of which waited for: 3 -> 1; matrix products, arithmetic and copies ran while one was open for 1% -> 0% of each run, Pallas kernels for 6% -> 50%
where the time goes in v2:
time: 236 us; the launch traced here: 235 us
  Pallas kernels  153 us (65%)
  waiting for transfers between devices  41.2 us (17%)
  blocking collectives  12.9 us (5%)
  local copies, waits for them, and re-layouts  12.8 us (5%)
  starting transfers between devices  12.6 us (5%)
    pallas_call x1, Pallas kernels, gather_weights(): pl.pallas_call(functools.partial(ring_kernel, chips), out_shape=[jax.Shap...  102 us
    all_to_all x1, waiting for transfers between devices, per_device(): lax.all_to_all(mixed, 'pair', split_axis=0, concat_axis=0, tiled=True)  41.2 us
    pallas_call x1, Pallas kernels, owner_attention(): pl.pallas_call(functools.partial(owner_kernel, per, kvw // hd, hd, hd **...  21.8 us
    pallas_call x2, Pallas kernels, project(): pl.pallas_call(functools.partial(project_kernel, hd), grid=(rows // block...  16.1 us
    all_to_all x1, blocking collectives, per_device(): lax.all_to_all(totals, 'pair', split_axis=0, concat_axis=0, tiled=True)  12.9 us
    unnamed x29, local copies, waits for them, and re-layouts  12.4 us
    pallas_call x1, Pallas kernels, combine(): pl.pallas_call(functools.partial(combine_kernel, per, plen, kvw // hd, hd...  12 us
    all_to_all x1, starting transfers between devices, per_device(): lax.all_to_all(outgoing, 'pair', split_axis=0, concat_axis=0, tiled=True)  6.69 us
  transfers between devices with their start and end apart: 2, of which 1 were waited for; matrix products, arithmetic and copies ran while one was open for 0% of the time, Pallas kernels for 50%

profile of v2, /device:TPU:13, one launch (start us, length us, event | category | flops | bytes accessed | tf_op | source)
XLA Modules:
  0.0 235.3 jit_solution(9912417291556350137)
XLA Ops:
  0.0 0.8 copy.12
  0.8 0.1 eq.34
  0.9 1.4 select_reduce_fusion
  2.4 0.5 convert_reduce_fusion
  2.8 0.1 select_reduce_fusion.4.idx_ref
  3.0 0.0 copy-start.7
  3.0 1.2 copy-done.7
  4.2 0.0 copy-start.13
  4.2 0.7 copy-done.13
  4.8 1.4 shard_map.100
  6.3 0.0 copy-start.1
  6.3 1.3 copy-done.1
  7.6 0.0 copy-start.4
  7.6 1.0 copy-done.4
  8.6 0.0 copy-start.8
  8.6 0.0 copy-start.9
  8.6 0.0 copy-start.12
  8.6 6.7 %all-to-all-start = ((bf16[32,256,128]{2,1,0:T(8,128)(2,1)}), bf16[32,256,128]{2,1,0:T(8,128)(2,1)S(1)}, u32[]{:S(2)}, u32[]{:S(2)}) async-start(bf16[32,256,128]{2,1,0:T(8,128)(2,1)} %copy-done.1), calls=%async_computation | async-start | bytes 4194304 | tf_op jit(solution)/shard_map/all_to_all | solution.py:354
  15.3 0.1 select_reduce_fusion.2
  15.5 0.1 copy.14
  15.5 0.1 max.7.len_ref
  15.6 0.1 copy.13
  15.7 0.1 reshape.148.slot_ref
  15.8 0.0 copy-done.8
  15.8 0.0 copy-done.9
  15.8 102.1 %shard_map.101 = (bf16[16,320,512]{2,1,0:T(8,128)(2,1)S(1)}, bf16[16,320,512]{2,1,0:T(8,128)(2,1)}) custom-call(bf16[320,512]{1,0:T(8,128)(2,1)S(1)} %copy-done.8, bf16[320,512]{1,0:T(8,128)(2,1)S(1)} %copy-done.9), custom_call_target="tpu_custom_call" | custom-call | tf_op jit(solution)/shard_map/pallas_call | solution.py:309
  117.9 0.0 copy-start
  117.9 2.3 copy-done
  120.2 0.0 copy-done.12
  120.2 10.6 %shard_map.103 = (bf16[512,512]{1,0:T(8,128)(2,1)S(1)}, bf16[512,512]{1,0:T(8,128)(2,1)S(1)}) custom-call(bf16[512,5120]{1,0:T(8,128)(2,1)} %bitcast.23, bf16[5120,512]{1,0:T(8,128)(2,1)} %bitcast.12, bf16[5120,512]{1,0:T(8,128)(2,1)} %bitcast.21, f32[1,128]{1,0:T(1,128)S(1)} %bitcast.18), custom_call_target="tpu_custom_call" | custom-call | tf_op jit(solution)/shard_map/pallas_call | solution.py:86
  130.8 0.0 all-to-all-done.q_ref
  130.8 21.8 %shard_map.104 = (bf16[32,256,128]{2,1,0:T(8,128)(2,1)S(1)}, f32[32,8,256]{2,1,0:T(8,128)S(1)}) custom-call(s32[32]{0:T(128)S(1)} %reshape.148.slot_ref, s32[32]{0:T(128)S(1)} %max.7.len_ref, bf16[32,256,128]{2,1,0:T(8,128)(2,1)S(1)} %all-to-all-done.q_ref, bf16[4,128,512]{2,1,0:T(8,128)(2,1)S(1)} %bitcast.16, bf16[4,128,512]{2,1,0:T(8,128)(2,1)S(1)} %bitcast.17), custom_call_target="tpu_custom_call" | custom-call | tf_op jit(solution)/shard_map/pallas_call | solution.py:135
  152.7 0.0 copy-start.2
  152.7 1.3 copy-done.2
  154.0 12.9 %all_to_all.15.t_ref = f32[32,8,256]{2,1,0:T(8,128)} all-to-all(f32[32,8,256]{2,1,0:T(8,128)S(1)} %get-tuple-element.24), channel_id=1, replica_groups=mesh['groups'=2,'pair'=16] {'pair'}, dimensions={0} | all-to-all | bytes 524288 | tf_op jit(solution)/shard_map/all_to_all | solution.py:368
  166.9 0.0 copy-start.3
  166.9 5.9 %all-to-all-start.1 = ((bf16[32,256,128]{2,1,0:T(8,128)(2,1)}), bf16[32,256,128]{2,1,0:T(8,128)(2,1)S(1)}, u32[]{:S(2)}, u32[]{:S(2)}) async-start(bf16[32,256,128]{2,1,0:T(8,128)(2,1)} %copy-done.2), calls=%async_computation.1 | async-start | bytes 4194304 | tf_op jit(solution)/shard_map/all_to_all | solution.py:367
  172.8 0.0 copy-done.3
  172.8 5.6 %shard_map.102 = (bf16[128,512]{1,0:T(8,128)(2,1)S(1)}, bf16[128,512]{1,0:T(8,128)(2,1)S(1)}) custom-call(bf16[128,5120]{1,0:T(8,128)(2,1)S(1)} %bitcast.14, bf16[5120,512]{1,0:T(8,128)(2,1)} %bitcast.13, bf16[5120,512]{1,0:T(8,128)(2,1)} %bitcast.22, f32[1,128]{1,0:T(1,128)S(1)} %bitcast.19), custom_call_target="tpu_custom_call" | custom-call | tf_op jit(solution)/shard_map/pallas_call | solution.py:86
  178.4 0.0 copy-start.10
  178.4 0.6 copy-done.10
  179.0 41.2 %all-to-all-done.1.in_ref = bf16[32,256,128]{2,1,0:T(8,128)(2,1)S(1)} async-done(((bf16[32,256,128]{2,1,0:T(8,128)(2,1)}), bf16[32,256,128]{2,1,0:T(8,128)(2,1)S(1)}, u32[]{:S(2)}, u32[]{:S(2)}) %all-to-all-start.1) | async-done | bytes 2097184 | tf_op jit(solution)/shard_map/all_to_all | solution.py:367
  220.2 0.0 copy-start.5
  220.2 1.2 copy-done.5
  221.4 0.0 copy-start.6
  221.4 0.9 copy-done.6
  222.4 0.0 copy-start.11
  222.4 0.9 copy-done.11
  223.3 12.0 %shard_map.105 = bf16[128,4096]{1,0:T(8,128)(2,1)} custom-call(s32[32]{0:T(128)S(1)} %add_bitcast_fusion.at_ref, bf16[16,256,128]{2,1,0:T(8,128)(2,1)S(1)} %copy-done.5, bf16[128,512]{1,0:T(8,128)(2,1)S(1)} %get-tuple-element.18.k_ref, bf16[128,512]{1,0:T(8,128)(2,1)S(1)} %copy-done.11, bf16[32,256,128]{2,1,0:T(8,128)(2,1)S(1)} %all-to-all-done.1.in_ref, ...), custom_call_target="tpu_custom_call" | custom-call | tf_op jit(solution)/shard_map/pallas_call | solution.py:196
  (6 shorter events, 0.1 us)
Async XLA Ops:
  3.0 1.2 copy-start.7
  4.2 0.7 copy-start.13
  6.3 1.3 copy-start.1
  7.6 1.0 copy-start.4
  8.6 7.2 %copy-start.8 = (bf16[320,512]{1,0:T(8,128)(2,1)S(1)}, bf16[320,512]{1,0:T(8,128)(2,1)}, u32[]{:S(2)}) copy-start(bf16[320,512]{1,0:T(8,128)(2,1)} %wk_ref.1) | copy-start | bytes 983044
  8.6 7.2 %copy-start.9 = (bf16[320,512]{1,0:T(8,128)(2,1)S(1)}, bf16[320,512]{1,0:T(8,128)(2,1)}, u32[]{:S(2)}) copy-start(bf16[320,512]{1,0:T(8,128)(2,1)} %wv_ref.1) | copy-start | bytes 983044
  8.6 111.6 %copy-start.12 = (f32[128]{0:T(128)S(1)}, f32[128]{0:T(128)}, u32[]{:S(2)}) copy-start(f32[128]{0:T(128)} %param.15) | copy-start | bytes 1540
  8.6 122.2 %all-to-all-start = ((bf16[32,256,128]{2,1,0:T(8,128)(2,1)}), bf16[32,256,128]{2,1,0:T(8,128)(2,1)S(1)}, u32[]{:S(2)}, u32[]{:S(2)}) async-start(bf16[32,256,128]{2,1,0:T(8,128)(2,1)} %copy-done.1), calls=%async_computation | async-start | bytes 4194304 | tf_op jit(solution)/shard_map/all_to_all | solution.py:354
  117.9 2.3 copy-start
  152.7 1.3 copy-start.2
  166.9 5.9 %copy-start.3 = (bf16[16,8,5120]{2,1,0:T(8,128)(2,1)S(1)}, bf16[16,8,5120]{2,1,0:T(8,128)(2,1)}, u32[]{:S(2)}) copy-start(bf16[16,8,5120]{2,1,0:T(8,128)(2,1)} %param.11) | copy-start | bytes 3932164
  166.9 53.3 %all-to-all-start.1 = ((bf16[32,256,128]{2,1,0:T(8,128)(2,1)}), bf16[32,256,128]{2,1,0:T(8,128)(2,1)S(1)}, u32[]{:S(2)}, u32[]{:S(2)}) async-start(bf16[32,256,128]{2,1,0:T(8,128)(2,1)} %copy-done.2), calls=%async_computation.1 | async-start | bytes 4194304 | tf_op jit(solution)/shard_map/all_to_all | solution.py:367
  178.4 0.7 copy-start.10
  220.2 1.2 copy-start.5
  221.4 0.9 copy-start.6
  222.4 0.9 copy-start.11

commit v3 on v2

--- a/solution.py
+++ b/solution.py
@@ -106,25 +106,66 @@
     return (numer / total).astype(jnp.bfloat16), total
 
 
-def owner_kernel(per, kvh, hd, scale, slot_ref, len_ref, q_ref, k_ref, v_ref, o_ref, t_ref):
+def owner_kernel(per, kvh, hd, scale, slot_ref, len_ref, q_ref, k_ref, v_ref, o_ref):
     step = pl.program_id(0)
     rows = q_ref.shape[1]
     each = rows // kvh
+    alen = k_ref.shape[1]
+    spots = [(slice(h * each, (h + 1) * each), slice(h * hd, (h + 1) * hd)) for h in range(kvh)]
     for e in range(per):
         ref = step * per + e
         row = slot_ref[ref]
         count = len_ref[ref]
-        totals = []
-        for h in range(kvh):
-            cols = slice(h * hd, (h + 1) * hd)
-            keys = k_ref[row, :, cols]
-            position = lax.broadcasted_iota(jnp.int32, (each, keys.shape[0]), 1)
-            mixed, total = attend(
-                q_ref[e, h * each : (h + 1) * each, :], keys, v_ref[row, :, cols], position < count, scale
-            )
-            o_ref[e, h * each : (h + 1) * each, :] = mixed
-            totals.append(jnp.broadcast_to(total, (each, hd)))
-        t_ref[e] = jnp.concatenate(totals, axis=0).T[:8]
+        scores = jnp.concatenate(
+            [
+                lax.dot_general(
+                    q_ref[e, at, :], k_ref[row, :, cols], (((1,), (1,)), ((), ())),
+                    preferred_element_type=jnp.float32,
+                )
+                for at, cols in spots
+            ],
+            axis=0,
+        )
+        position = lax.broadcasted_iota(jnp.int32, (rows, alen), 1)
+        weights = jnp.where(position < count, jnp.exp(scores * scale), 0.0)
+        total = jnp.sum(weights, axis=-1, keepdims=True)
+        rounded = weights.astype(jnp.bfloat16)
+        numer = jnp.concatenate(
+            [
+                jnp.dot(rounded[at], v_ref[row, :, cols], preferred_element_type=jnp.float32)
+                for at, cols in spots
+            ],
+            axis=0,
+        )
+        o_ref[e, :rows, :] = (numer / total).astype(jnp.bfloat16)
+        o_ref[e, rows:, :] = pack_totals(jnp.broadcast_to(total, (rows, hd)))
+
+
+def pack_totals(total):
+    rows, hd = total.shape
+    flat = total.T[:16]
+    left = [flat[:, i * hd : (i + 1) * hd] for i in range(rows // hd)]
+    place = lax.broadcasted_iota(jnp.int32, (16, hd), 0)
+    packed = jnp.zeros((16, hd), jnp.float32)
+    at = 0
+    for _ in range(3):
+        for i in range(len(left)):
+            term = left[i].astype(jnp.bfloat16).astype(jnp.float32)
+            packed = jnp.where(place == at, term, packed)
+            left[i] = left[i] - term
+            at += 1
+    return packed.astype(jnp.bfloat16)
+
+
+def unpack_totals(packed, rows):
+    hd = packed.shape[1]
+    terms = packed.astype(jnp.float32)
+    count = rows // hd
+    flat = [
+        terms[i : i + 1] + terms[count + i : count + i + 1] + terms[2 * count + i : 2 * count + i + 1]
+        for i in range(count)
+    ]
+    return jnp.concatenate([jnp.broadcast_to(f, (hd, hd)).T for f in flat], axis=0)
 
 
 def owner_attention(slot, lens, q, keys, values, hd):
@@ -142,20 +183,14 @@
                 spec(keys.shape, lambda i, *_: (0, 0, 0)),
                 spec(keys.shape, lambda i, *_: (0, 0, 0)),
             ],
-            out_specs=[
-                spec((per, rows, hd), lambda i, *_: (i, 0, 0)),
-                spec((per, 8, rows), lambda i, *_: (i, 0, 0)),
-            ],
+            out_specs=spec((per, rows + 16, hd), lambda i, *_: (i, 0, 0)),
         ),
-        out_shape=[
-            jax.ShapeDtypeStruct((slots, rows, hd), jnp.bfloat16),
-            jax.ShapeDtypeStruct((slots, 8, rows), jnp.float32),
-        ],
+        out_shape=jax.ShapeDtypeStruct((slots, rows + 16, hd), jnp.bfloat16),
         compiler_params=pltpu.CompilerParams(vmem_limit_bytes=LIMIT),
     )(slot, lens, q, keys, values)
 
 
-def combine_kernel(per, plen, kvh, hd, scale, at_ref, q_ref, k_ref, v_ref, in_ref, t_ref, o_ref):
+def combine_kernel(per, plen, kvh, hd, scale, at_ref, q_ref, k_ref, v_ref, in_ref, o_ref):
     step = pl.program_id(0)
     rows = q_ref.shape[1]
     each = rows // kvh
@@ -178,8 +213,8 @@
         denom = jnp.concatenate(denoms, axis=0)
         for side in range(2):
             at = at_ref[pair * 2 + side]
-            total = jnp.broadcast_to(t_ref[at][:1], (hd, rows)).T
-            numer = numer + total * in_ref[at].astype(jnp.float32)
+            total = unpack_totals(in_ref[at, rows:, :], rows)
+            numer = numer + total * in_ref[at, :rows, :].astype(jnp.float32)
             denom = denom + total
         results.append(numer / denom)
     for head in range(rows // plen):
@@ -187,7 +222,7 @@
         o_ref[:, head * hd : (head + 1) * hd] = block.astype(jnp.bfloat16)
 
 
-def combine(at, q, keys, values, incoming, totals, plen, hd):
+def combine(at, q, keys, values, incoming, plen, hd):
     pairs, rows, _ = q.shape
     slots = incoming.shape[0]
     kvw = keys.shape[1]
@@ -203,21 +238,24 @@
                 pl.BlockSpec(keys.shape, lambda i, *_: (0, 0)),
                 pl.BlockSpec(keys.shape, lambda i, *_: (0, 0)),
                 pl.BlockSpec(incoming.shape, lambda i, *_: (0, 0, 0)),
-                pl.BlockSpec(totals.shape, lambda i, *_: (0, 0, 0)),
             ],
             out_specs=pl.BlockSpec((per * plen, heads * hd), lambda i, *_: (i, 0)),
         ),
         out_shape=jax.ShapeDtypeStruct((pairs * plen, heads * hd), jnp.bfloat16),
         compiler_params=pltpu.CompilerParams(vmem_limit_bytes=LIMIT),
-    )(at, q, keys, values, incoming, totals)
-
-
-def ring_kernel(chips, wk_ref, wv_ref, ok_ref, ov_ref, own_sem, ring_send, ring_recv, side_send, side_recv):
+    )(at, q, keys, values, incoming)
+
+
+def ring_kernel(
+    chips, seg, wk_ref, wv_ref, ok_ref, ov_ref,
+    own_sem, ring_send, ring_recv, side_send, side_recv, swap_send, swap_recv, late_send, late_recv,
+):
     me = lax.axis_index("pair")
     group = lax.axis_index("groups")
     depth = wk_ref.shape[0]
     chip, core = me // 2, me % 2
     even = chip % 2
+    odd_group = group % 2
     position = (1 - even) * (chip // 2) + even * (chips - 1 - chip // 2)
 
     def chip_at(place):
@@ -225,15 +263,16 @@
         back = place // (chips // 2)
         return (1 - back) * 2 * place + back * (2 * (chips - 1 - place) + 1)
 
-    right = chip_at(position + 1) * 2 + core
-    left = chip_at(position - 1) * 2 + core
-    sibling = chip * 2 + 1 - core
+    right = (group, chip_at(position + 1) * 2 + core)
+    left = (group, chip_at(position - 1) * 2 + core)
+    sibling = (group, chip * 2 + 1 - core)
+    twin = (group + 1 - 2 * odd_group, me)
     partners = (right, left)
     mesh_id = pl.DeviceIdType.MESH
 
     barrier = pltpu.get_barrier_semaphore()
-    for other in (right, left, sibling):
-        pl.semaphore_signal(barrier, inc=1, device_id=(group, other), device_id_type=mesh_id)
+    for other in (right, left, sibling, twin):
+        pl.semaphore_signal(barrier, inc=1, device_id=other, device_id_type=mesh_id)
     own = []
     outs = (ok_ref, ov_ref)
     for w, (src, out) in enumerate(((wk_ref, ok_ref), (wv_ref, ov_ref))):
@@ -242,57 +281,80 @@
         own.append(copy)
     for copy in own:
         copy.wait()
-    pl.semaphore_wait(barrier, 3)
-
-    def piece(w, step):
-        return chip_at(position - step if w == 0 else position + step) * 2 + core
-
-    def ring(w, step):
-        block = outs[w].at[piece(w, step)]
+    pl.semaphore_wait(barrier, 4)
+
+    ringed = pl.ds(pl.multiple_of(odd_group * seg, 16), depth - seg)
+    mine = pl.ds(pl.multiple_of(odd_group * (depth - seg), 16), seg)
+    other_rows = pl.ds(pl.multiple_of((1 - odd_group) * (depth - seg), 16), seg)
+
+    def piece(w, step, on):
+        return chip_at(position - step if w == 0 else position + step) * 2 + on
+
+    def remote(block, send, recv, target):
         return pltpu.make_async_remote_copy(
-            src_ref=block, dst_ref=block, send_sem=ring_send.at[w, step], recv_sem=ring_recv.at[w, step],
-            device_id=(group, partners[w]), device_id_type=mesh_id,
+            src_ref=block, dst_ref=block, send_sem=send, recv_sem=recv, device_id=target, device_id_type=mesh_id
         )
 
-    def arriving(w, step):
-        block = outs[w].at[piece(w, step + 1)]
-        return pltpu.make_async_remote_copy(
-            src_ref=block, dst_ref=block, send_sem=ring_send.at[w, step], recv_sem=ring_recv.at[w, step],
-            device_id=(group, partners[w]), device_id_type=mesh_id,
-        )
-
-    def across(w, step, mine):
-        block = outs[w].at[piece(w, step) if mine else chip_at(position - step if w == 0 else position + step) * 2 + 1 - core]
-        return pltpu.make_async_remote_copy(
-            src_ref=block, dst_ref=block, send_sem=side_send.at[w, step], recv_sem=side_recv.at[w, step],
-            device_id=(group, sibling), device_id_type=mesh_id,
-        )
+    def ring(w, step, arriving=0):
+        block = outs[w].at[piece(w, step + arriving, core), ringed]
+        return remote(block, ring_send.at[w, step], ring_recv.at[w, step], partners[w])
+
+    def side(w, step, on):
+        block = outs[w].at[piece(w, step, on), ringed]
+        return remote(block, side_send.at[w, step], side_recv.at[w, step], sibling)
+
+    def swap(w, step, rows):
+        block = outs[w].at[piece(w, step, core), rows]
+        return remote(block, swap_send.at[w, step], swap_recv.at[w, step], twin)
+
+    def late(w, step, on):
+        block = outs[w].at[piece(w, step, on), other_rows]
+        return remote(block, late_send.at[w, step], late_recv.at[w, step], sibling)
 
     for w in range(2):
         ring(w, 0).start()
-        across(w, 0, True).start()
+    for w in range(2):
+        side(w, 0, core).start()
+        late(w, 0, core).start()
 
     def body(step, carry):
         for w in range(2):
-            arriving(w, step - 1).wait_recv()
+            ring(w, step - 1, 1).wait_recv()
 
             @pl.when(step < chips - 1)
             def _():
                 ring(w, step).start()
 
-            across(w, step, True).start()
+            swap(w, step, mine).start()
+            side(w, step, core).start()
+
+        @pl.when(step > 1)
+        def _():
+            for w in range(2):
+                swap(w, step - 1, other_rows).wait_recv()
+                late(w, step - 1, core).start()
+
         return carry
 
     lax.fori_loop(1, chips, body, 0)
+    for w in range(2):
+        swap(w, chips - 1, other_rows).wait_recv()
+        late(w, chips - 1, core).start()
 
     def drain(step, carry):
         for w in range(2):
-            across(w, step, True).wait_send()
-            across(w, step, False).wait_recv()
+            side(w, step, core).wait_send()
+            side(w, step, 1 - core).wait_recv()
+            late(w, step, core).wait_send()
+            late(w, step, 1 - core).wait_recv()
 
             @pl.when(step < chips - 1)
             def _():
                 ring(w, step).wait_send()
+
+            @pl.when(step > 0)
+            def _():
+                swap(w, step, mine).wait_send()
 
         return carry
 
@@ -305,13 +367,14 @@
     if not USE_RING:
         return tuple(lax.all_gather(w, "pair", axis=0, tiled=True) for w in (w_key, w_value))
     chips = peers // 2
+    seg = max(1, round(depth // 16 * 0.35)) * 16
     hbm = pl.BlockSpec(memory_space=pl.ANY)
     out = pl.pallas_call(
-        functools.partial(ring_kernel, chips),
+        functools.partial(ring_kernel, chips, seg),
         out_shape=[jax.ShapeDtypeStruct((peers, depth, kvw), jnp.bfloat16)] * 2,
         in_specs=[hbm] * 2,
         out_specs=[hbm] * 2,
-        scratch_shapes=[pltpu.SemaphoreType.DMA((2,))] + [pltpu.SemaphoreType.DMA((2, chips))] * 4,
+        scratch_shapes=[pltpu.SemaphoreType.DMA((2,))] + [pltpu.SemaphoreType.DMA((2, chips))] * 8,
         compiler_params=pltpu.CompilerParams(
             collective_id=0, has_side_effects=True, vmem_limit_bytes=LIMIT
         ),
@@ -356,7 +419,7 @@
     answer_keys, answer_values = project(
         answer_states.reshape(ans_dev * ans_len, width), key_full, value_full, key_gain
     )
-    mixed, totals = owner_attention(
+    mixed = owner_attention(
         slot_local,
         slot_lens,
         asked,
@@ -365,12 +428,11 @@
         head_dim,
     )
     mixed_in = lax.all_to_all(mixed, "pair", split_axis=0, concat_axis=0, tiled=True)
-    totals_in = lax.all_to_all(totals, "pair", split_axis=0, concat_axis=0, tiled=True)
     prompt_keys, prompt_values = project(
         prompt_states.reshape(pairs_dev * prompt_len, width), key_full, value_full, key_gain
     )
     out = combine(
-        fetch_index, query_own, prompt_keys, prompt_values, mixed_in, totals_in, prompt_len, head_dim
+        fetch_index, query_own, prompt_keys, prompt_values, mixed_in, prompt_len, head_dim
     )
     return out.reshape(queries.shape)
 

time: 236 us -> 206 us (0.87)
  Pallas kernels: 153 us -> 131 us
  blocking collectives: 12.9 us -> 0 us
  starting transfers between devices: 12.6 us -> 15 us
    all_to_all x1 -> x0, blocking collectives: 12.9 us -> none  [per_device(): lax.all_to_all(totals, 'pair', split_axis=0, concat_axis=0, tiled=True)]
    pallas_call x1, Pallas kernels: 21.8 us -> 8.95 us  [owner_attention(): pl.pallas_call(functools.partial(owner_kernel, per, kvw // hd, hd, hd **...]
    pallas_call x1, Pallas kernels: 102 us -> 92.4 us  [gather_weights(): pl.pallas_call(functools.partial(ring_kernel, chips, seg), out_shape=[jax...]
    all_to_all x1, starting transfers between devices: 5.88 us -> 8.35 us  [per_device(): lax.all_to_all(mixed, 'pair', split_axis=0, concat_axis=0, tiled=True)]
    unnamed x29 -> x31, local copies, waits for them, and re-layouts: 12.4 us -> 13 us
  transfers between devices with their start and end apart: 2 -> 2, of which waited for: 1 -> 1; matrix products, arithmetic and copies ran while one was open for 0% -> 0% of each run, Pallas kernels for 50% -> 53%
where the time goes in v3:
time: 206 us; the launch traced here: 205 us
  Pallas kernels  131 us (64%)
  waiting for transfers between devices  43.3 us (21%)
  starting transfers between devices  15 us (7%)
  local copies, waits for them, and re-layouts  13.5 us (7%)
  other arithmetic  2.17 us (1%)
    pallas_call x1, Pallas kernels, gather_weights(): pl.pallas_call(functools.partial(ring_kernel, chips, seg), out_shape=[jax...  92.4 us
    all_to_all x1, waiting for transfers between devices, per_device(): lax.all_to_all(mixed, 'pair', split_axis=0, concat_axis=0, tiled=True)  43.3 us
    pallas_call x2, Pallas kernels, project(): pl.pallas_call(functools.partial(project_kernel, hd), grid=(rows // block...  16.1 us
    unnamed x31, local copies, waits for them, and re-layouts  13 us
    pallas_call x1, Pallas kernels, combine(): pl.pallas_call(functools.partial(combine_kernel, per, plen, kvw // hd, hd...  12 us
    pallas_call x1, Pallas kernels, owner_attention(): pl.pallas_call(functools.partial(owner_kernel, per, kvw // hd, hd, hd **...  8.95 us
    all_to_all x1, starting transfers between devices, per_device(): lax.all_to_all(mixed, 'pair', split_axis=0, concat_axis=0, tiled=True)  8.35 us
    all_to_all x1, starting transfers between devices, per_device(): lax.all_to_all(outgoing, 'pair', split_axis=0, concat_axis=0, tiled=True)  6.69 us
  transfers between devices with their start and end apart: 2, of which 1 were waited for; matrix products, arithmetic and copies ran while one was open for 0% of the time, Pallas kernels for 53%

profile of v3, /device:TPU:13, one launch (start us, length us, event | category | flops | bytes accessed | tf_op | source)
XLA Modules:
  0.0 205.2 jit_solution(148916422892159924)
XLA Ops:
  0.0 0.8 copy.12
  0.8 0.1 eq.34
  0.9 1.4 select_reduce_fusion
  2.4 0.5 convert_reduce_fusion
  2.8 0.1 select_reduce_fusion.4.idx_ref
  3.0 0.0 copy-start.6
  3.0 1.2 copy-done.6
  4.2 0.0 copy-start.14
  4.2 0.7 copy-done.14
  4.8 1.4 shard_map.100
  6.3 0.0 copy-start.2
  6.3 1.3 copy-done.2
  7.6 0.0 copy-start.4
  7.6 1.0 copy-done.4
  8.6 0.0 copy-start.7
  8.6 0.0 copy-start.8
  8.6 0.0 copy-start.13
  8.6 6.7 %all-to-all-start = ((bf16[32,256,128]{2,1,0:T(8,128)(2,1)}), bf16[32,256,128]{2,1,0:T(8,128)(2,1)S(1)}, u32[]{:S(2)}, u32[]{:S(2)}) async-start(bf16[32,256,128]{2,1,0:T(8,128)(2,1)} %copy-done.2), calls=%async_computation | async-start | bytes 4194304 | tf_op jit(solution)/shard_map/all_to_all | solution.py:417
  15.3 0.1 select_reduce_fusion.2
  15.5 0.1 copy.14
  15.5 0.1 max.7.len_ref
  15.6 0.1 copy.13
  15.7 0.1 reshape.148.slot_ref
  15.8 0.0 copy-done.7
  15.8 0.0 copy-done.8
  15.8 92.4 %shard_map.101 = (bf16[16,320,512]{2,1,0:T(8,128)(2,1)S(1)}, bf16[16,320,512]{2,1,0:T(8,128)(2,1)}) custom-call(bf16[320,512]{1,0:T(8,128)(2,1)S(1)} %copy-done.7, bf16[320,512]{1,0:T(8,128)(2,1)S(1)} %copy-done.8), custom_call_target="tpu_custom_call" | custom-call | tf_op jit(solution)/shard_map/pallas_call | solution.py:372
  108.3 0.0 copy-start
  108.3 2.3 %copy-done = bf16[16,320,512]{2,1,0:T(8,128)(2,1)} copy-done((bf16[16,320,512]{2,1,0:T(8,128)(2,1)}, bf16[16,320,512]{2,1,0:T(8,128)(2,1)S(1)}, u32[]{:S(2)}) %copy-start) | copy-done | bytes 5242904
  110.6 0.0 copy-done.13
  110.6 10.6 %shard_map.103 = (bf16[512,512]{1,0:T(8,128)(2,1)S(1)}, bf16[512,512]{1,0:T(8,128)(2,1)S(1)}) custom-call(bf16[512,5120]{1,0:T(8,128)(2,1)} %bitcast.23, bf16[5120,512]{1,0:T(8,128)(2,1)} %bitcast.12, bf16[5120,512]{1,0:T(8,128)(2,1)} %bitcast.21, f32[1,128]{1,0:T(1,128)S(1)} %bitcast.18), custom_call_target="tpu_custom_call" | custom-call | tf_op jit(solution)/shard_map/pallas_call | solution.py:86
  121.2 0.0 all-to-all-done.q_ref
  121.2 9.0 %shard_map.104 = bf16[32,272,128]{2,1,0:T(8,128)(2,1)S(1)} custom-call(s32[32]{0:T(128)S(1)} %reshape.148.slot_ref, s32[32]{0:T(128)S(1)} %max.7.len_ref, bf16[32,256,128]{2,1,0:T(8,128)(2,1)S(1)} %all-to-all-done.q_ref, bf16[4,128,512]{2,1,0:T(8,128)(2,1)S(1)} %bitcast.16, bf16[4,128,512]{2,1,0:T(8,128)(2,1)S(1)} %bitcast.17), custom_call_target="tpu_custom_call" | custom-call | tf_op jit(solution)/shard_map/pallas_call | solution.py:176
  130.2 0.0 copy-start.1
  130.2 1.4 copy-done.1
  131.6 0.0 copy-start.3
  131.6 8.4 %all-to-all-start.1 = ((bf16[32,272,128]{2,1,0:T(8,128)(2,1)}), bf16[32,272,128]{2,1,0:T(8,128)(2,1)S(1)}, u32[]{:S(2)}, u32[]{:S(2)}) async-start(bf16[32,272,128]{2,1,0:T(8,128)(2,1)} %copy-done.1), calls=%async_computation.1 | async-start | bytes 4456448 | tf_op jit(solution)/shard_map/all_to_all | solution.py:430
  139.9 0.0 copy-done.3
  139.9 5.6 %shard_map.102 = (bf16[128,512]{1,0:T(8,128)(2,1)S(1)}, bf16[128,512]{1,0:T(8,128)(2,1)S(1)}) custom-call(bf16[128,5120]{1,0:T(8,128)(2,1)S(1)} %bitcast.14, bf16[5120,512]{1,0:T(8,128)(2,1)} %bitcast.13, bf16[5120,512]{1,0:T(8,128)(2,1)} %bitcast.22, f32[1,128]{1,0:T(1,128)S(1)} %bitcast.19), custom_call_target="tpu_custom_call" | custom-call | tf_op jit(solution)/shard_map/pallas_call | solution.py:86
  145.5 0.0 copy-start.9
  145.5 0.6 copy-done.9
  146.2 0.0 copy-start.11
  146.2 0.7 copy-done.11
  146.8 43.3 %all-to-all-done.1.in_ref = bf16[32,272,128]{2,1,0:T(8,128)(2,1)S(1)} async-done(((bf16[32,272,128]{2,1,0:T(8,128)(2,1)}), bf16[32,272,128]{2,1,0:T(8,128)(2,1)S(1)}, u32[]{:S(2)}, u32[]{:S(2)}) %all-to-all-start.1) | async-done | bytes 2228256 | tf_op jit(solution)/shard_map/all_to_all | solution.py:430
  190.1 0.0 copy-start.5
  190.1 1.2 copy-done.5
  191.4 0.0 copy-start.10
  191.4 0.9 copy-done.10
  192.3 0.0 copy-start.12
  192.3 0.9 copy-done.12
  193.2 12.0 %shard_map.105 = bf16[128,4096]{1,0:T(8,128)(2,1)} custom-call(s32[32]{0:T(128)S(1)} %add_bitcast_fusion.at_ref, bf16[16,256,128]{2,1,0:T(8,128)(2,1)S(1)} %copy-done.5, bf16[128,512]{1,0:T(8,128)(2,1)S(1)} %copy-done.10, bf16[128,512]{1,0:T(8,128)(2,1)S(1)} %copy-done.12, bf16[32,272,128]{2,1,0:T(8,128)(2,1)S(1)} %all-to-all-done.1.in_ref), custom_call_target="tpu_custom_call" | custom-call | tf_op jit(solution)/shard_map/pallas_call | solution.py:231
  (6 shorter events, 0.1 us)
Async XLA Ops:
  3.0 1.2 copy-start.6
  4.2 0.7 copy-start.14
  6.3 1.3 copy-start.2
  7.6 1.0 copy-start.4
  8.6 7.2 %copy-start.7 = (bf16[320,512]{1,0:T(8,128)(2,1)S(1)}, bf16[320,512]{1,0:T(8,128)(2,1)}, u32[]{:S(2)}) copy-start(bf16[320,512]{1,0:T(8,128)(2,1)} %wk_ref.1) | copy-start | bytes 983044
  8.6 7.2 %copy-start.8 = (bf16[320,512]{1,0:T(8,128)(2,1)S(1)}, bf16[320,512]{1,0:T(8,128)(2,1)}, u32[]{:S(2)}) copy-start(bf16[320,512]{1,0:T(8,128)(2,1)} %wv_ref.1) | copy-start | bytes 983044
  8.6 102.0 %copy-start.13 = (f32[128]{0:T(128)S(1)}, f32[128]{0:T(128)}, u32[]{:S(2)}) copy-start(f32[128]{0:T(128)} %param.15) | copy-start | bytes 1540
  8.6 112.6 %all-to-all-start = ((bf16[32,256,128]{2,1,0:T(8,128)(2,1)}), bf16[32,256,128]{2,1,0:T(8,128)(2,1)S(1)}, u32[]{:S(2)}, u32[]{:S(2)}) async-start(bf16[32,256,128]{2,1,0:T(8,128)(2,1)} %copy-done.2), calls=%async_computation | async-start | bytes 4194304 | tf_op jit(solution)/shard_map/all_to_all | solution.py:417
  108.3 2.3 %copy-start = (bf16[16,320,512]{2,1,0:T(8,128)(2,1)}, bf16[16,320,512]{2,1,0:T(8,128)(2,1)S(1)}, u32[]{:S(2)}) copy-start(bf16[16,320,512]{2,1,0:T(8,128)(2,1)S(1)} %get-tuple-element.14) | copy-start | bytes 15728644
  130.2 1.4 copy-start.1
  131.6 8.4 %copy-start.3 = (bf16[16,8,5120]{2,1,0:T(8,128)(2,1)S(1)}, bf16[16,8,5120]{2,1,0:T(8,128)(2,1)}, u32[]{:S(2)}) copy-start(bf16[16,8,5120]{2,1,0:T(8,128)(2,1)} %param.11) | copy-start | bytes 3932164
  131.6 58.6 %all-to-all-start.1 = ((bf16[32,272,128]{2,1,0:T(8,128)(2,1)}), bf16[32,272,128]{2,1,0:T(8,128)(2,1)S(1)}, u32[]{:S(2)}, u32[]{:S(2)}) async-start(bf16[32,272,128]{2,1,0:T(8,128)(2,1)} %copy-done.1), calls=%async_computation.1 | async-start | bytes 4456448 | tf_op jit(solution)/shard_map/all_to_all | solution.py:430
  145.5 0.7 copy-start.9
  146.2 0.7 copy-start.11
  190.1 1.2 copy-start.5
  191.4 0.9 copy-start.10
  192.3 0.9 copy-start.12

commit v4 on v3

--- a/solution.py
+++ b/solution.py
@@ -96,14 +96,6 @@
         out_specs=[pl.BlockSpec((block, kvw), lambda i: (i, 0))] * 2,
         compiler_params=pltpu.CompilerParams(vmem_limit_bytes=LIMIT),
     )(x, wk, wv, gain.reshape(1, hd))
-
-
-def attend(q, k, v, valid, scale):
-    scores = lax.dot_general(q, k, (((1,), (1,)), ((), ())), preferred_element_type=jnp.float32) * scale
-    weights = jnp.where(valid, jnp.exp(scores), 0.0)
-    total = jnp.sum(weights, axis=-1, keepdims=True)
-    numer = jnp.dot(weights.astype(jnp.bfloat16), v, preferred_element_type=jnp.float32)
-    return (numer / total).astype(jnp.bfloat16), total
 
 
 def owner_kernel(per, kvh, hd, scale, slot_ref, len_ref, q_ref, k_ref, v_ref, o_ref):
@@ -190,29 +182,64 @@
     )(slot, lens, q, keys, values)
 
 
-def combine_kernel(per, plen, kvh, hd, scale, at_ref, q_ref, k_ref, v_ref, in_ref, o_ref):
+def prompt_kernel(per, plen, kvh, hd, scale, q_ref, k_ref, v_ref, n_ref, t_ref):
     step = pl.program_id(0)
     rows = q_ref.shape[1]
     each = rows // kvh
     keys_count = k_ref.shape[0]
+    spots = [(slice(h * each, (h + 1) * each), slice(h * hd, (h + 1) * hd)) for h in range(kvh)]
+    for e in range(per):
+        pair = step * per + e
+        place = lax.broadcasted_iota(jnp.int32, (rows, keys_count), 1)
+        token = lax.broadcasted_iota(jnp.int32, (rows, keys_count), 0) % plen
+        valid = (place >= pair * plen) & (place <= pair * plen + token)
+        scores = jnp.concatenate(
+            [
+                lax.dot_general(
+                    q_ref[e, at, :], k_ref[:, cols], (((1,), (1,)), ((), ())),
+                    preferred_element_type=jnp.float32,
+                )
+                for at, cols in spots
+            ],
+            axis=0,
+        )
+        weights = jnp.where(valid, jnp.exp(scores * scale), 0.0)
+        total = jnp.sum(weights, axis=-1, keepdims=True)
+        rounded = weights.astype(jnp.bfloat16)
+        numer = jnp.concatenate(
+            [jnp.dot(rounded[at], v_ref[:, cols], preferred_element_type=jnp.float32) for at, cols in spots],
+            axis=0,
+        )
+        mixed = (numer / total).astype(jnp.bfloat16).astype(jnp.float32)
+        n_ref[e] = total * mixed
+        t_ref[e] = jnp.broadcast_to(total, (rows, hd))
+
+
+def prompt_attention(q, keys, values, plen, hd):
+    pairs, rows, _ = q.shape
+    kvw = keys.shape[1]
+    per = 4
+    block = pl.BlockSpec((per, rows, hd), lambda i: (i, 0, 0))
+    full = pl.BlockSpec(keys.shape, lambda i: (0, 0))
+    return pl.pallas_call(
+        functools.partial(prompt_kernel, per, plen, kvw // hd, hd, hd ** (-0.5)),
+        grid=(pairs // per,),
+        in_specs=[block, full, full],
+        out_specs=[block] * 2,
+        out_shape=[jax.ShapeDtypeStruct((pairs, rows, hd), jnp.float32)] * 2,
+        compiler_params=pltpu.CompilerParams(vmem_limit_bytes=LIMIT),
+    )(q, keys, values)
+
+
+def combine_kernel(per, plen, hd, at_ref, n_ref, t_ref, in_ref, o_ref):
+    step = pl.program_id(0)
+    rows = n_ref.shape[1]
     results = []
     for e in range(per):
-        pair = step * per + e
-        place = lax.broadcasted_iota(jnp.int32, (each, keys_count), 1)
-        token = lax.broadcasted_iota(jnp.int32, (each, keys_count), 0) % plen
-        valid = (place // plen == pair) & (place % plen <= token)
-        numers, denoms = [], []
-        for h in range(kvh):
-            cols = slice(h * hd, (h + 1) * hd)
-            mixed, total = attend(
-                q_ref[e, h * each : (h + 1) * each, :], k_ref[:, cols], v_ref[:, cols], valid, scale
-            )
-            numers.append(total * mixed.astype(jnp.float32))
-            denoms.append(jnp.broadcast_to(total, (each, hd)))
-        numer = jnp.concatenate(numers, axis=0)
-        denom = jnp.concatenate(denoms, axis=0)
+        numer = n_ref[e]
+        denom = t_ref[e]
         for side in range(2):
-            at = at_ref[pair * 2 + side]
+            at = at_ref[(step * per + e) * 2 + side]
             total = unpack_totals(in_ref[at, rows:, :], rows)
             numer = numer + total * in_ref[at, :rows, :].astype(jnp.float32)
             denom = denom + total
@@ -222,28 +249,22 @@
         o_ref[:, head * hd : (head + 1) * hd] = block.astype(jnp.bfloat16)
 
 
-def combine(at, q, keys, values, incoming, plen, hd):
-    pairs, rows, _ = q.shape
-    slots = incoming.shape[0]
-    kvw = keys.shape[1]
+def combine(at, numer, denom, incoming, plen, hd):
+    pairs, rows, _ = numer.shape
     per = 4
     heads = rows // plen
+    block = pl.BlockSpec((per, rows, hd), lambda i, *_: (i, 0, 0))
     return pl.pallas_call(
-        functools.partial(combine_kernel, per, plen, kvw // hd, hd, hd ** (-0.5)),
+        functools.partial(combine_kernel, per, plen, hd),
         grid_spec=pltpu.PrefetchScalarGridSpec(
             num_scalar_prefetch=1,
             grid=(pairs // per,),
-            in_specs=[
-                pl.BlockSpec((per, rows, hd), lambda i, *_: (i, 0, 0)),
-                pl.BlockSpec(keys.shape, lambda i, *_: (0, 0)),
-                pl.BlockSpec(keys.shape, lambda i, *_: (0, 0)),
-                pl.BlockSpec(incoming.shape, lambda i, *_: (0, 0, 0)),
-            ],
+            in_specs=[block, block, pl.BlockSpec(incoming.shape, lambda i, *_: (0, 0, 0))],
             out_specs=pl.BlockSpec((per * plen, heads * hd), lambda i, *_: (i, 0)),
         ),
         out_shape=jax.ShapeDtypeStruct((pairs * plen, heads * hd), jnp.bfloat16),
         compiler_params=pltpu.CompilerParams(vmem_limit_bytes=LIMIT),
-    )(at, q, keys, values, incoming)
+    )(at, numer, denom, incoming)
 
 
 def ring_kernel(
@@ -283,7 +304,11 @@
         copy.wait()
     pl.semaphore_wait(barrier, 4)
 
-    ringed = pl.ds(pl.multiple_of(odd_group * seg, 16), depth - seg)
+    first = ((depth - seg) // 16 + 1) // 2 * 16
+    chunks = tuple(
+        pl.ds(pl.multiple_of(odd_group * seg + start, 16), size)
+        for start, size in ((0, first), (first, depth - seg - first))
+    )
     mine = pl.ds(pl.multiple_of(odd_group * (depth - seg), 16), seg)
     other_rows = pl.ds(pl.multiple_of((1 - odd_group) * (depth - seg), 16), seg)
 
@@ -295,13 +320,15 @@
             src_ref=block, dst_ref=block, send_sem=send, recv_sem=recv, device_id=target, device_id_type=mesh_id
         )
 
-    def ring(w, step, arriving=0):
-        block = outs[w].at[piece(w, step + arriving, core), ringed]
-        return remote(block, ring_send.at[w, step], ring_recv.at[w, step], partners[w])
-
-    def side(w, step, on):
-        block = outs[w].at[piece(w, step, on), ringed]
-        return remote(block, side_send.at[w, step], side_recv.at[w, step], sibling)
+    def ring(w, step, c, arriving=0):
+        block = outs[w].at[piece(w, step + arriving, core), chunks[c]]
+        at = 2 * step + c
+        return remote(block, ring_send.at[w, at], ring_recv.at[w, at], partners[w])
+
+    def side(w, step, c, on):
+        block = outs[w].at[piece(w, step, on), chunks[c]]
+        at = 2 * step + c
+        return remote(block, side_send.at[w, at], side_recv.at[w, at], sibling)
 
     def swap(w, step, rows):
         block = outs[w].at[piece(w, step, core), rows]
@@ -311,46 +338,59 @@
         block = outs[w].at[piece(w, step, on), other_rows]
         return remote(block, late_send.at[w, step], late_recv.at[w, step], sibling)
 
+    both = [(c, w) for c in range(2) for w in range(2)]
+    for c, w in both:
+        ring(w, 0, c).start()
+    for c, w in both:
+        side(w, 0, c, core).start()
     for w in range(2):
-        ring(w, 0).start()
-    for w in range(2):
-        side(w, 0, core).start()
         late(w, 0, core).start()
 
+    def hand_over(step):
+        for w in range(2):
+            swap(w, step, other_rows).wait_recv()
+            late(w, step, core).start()
+
+    lag = 3
+
     def body(step, carry):
-        for w in range(2):
-            ring(w, step - 1, 1).wait_recv()
+        for c, w in both:
+            ring(w, step - 1, c, 1).wait_recv()
 
             @pl.when(step < chips - 1)
             def _():
-                ring(w, step).start()
-
+                ring(w, step, c).start()
+
+            side(w, step, c, core).start()
+        for w in range(2):
             swap(w, step, mine).start()
-            side(w, step, core).start()
-
-        @pl.when(step > 1)
+
+        @pl.when(step > lag)
         def _():
-            for w in range(2):
-                swap(w, step - 1, other_rows).wait_recv()
-                late(w, step - 1, core).start()
+            hand_over(step - lag)
 
         return carry
 
     lax.fori_loop(1, chips, body, 0)
-    for w in range(2):
-        swap(w, chips - 1, other_rows).wait_recv()
-        late(w, chips - 1, core).start()
+
+    def finish(step, carry):
+        hand_over(step)
+        return carry
+
+    lax.fori_loop(chips - lag, chips, finish, 0)
 
     def drain(step, carry):
+        for c, w in both:
+            side(w, step, c, core).wait_send()
+            side(w, step, c, 1 - core).wait_recv()
+
+            @pl.when(step < chips - 1)
+            def _():
+                ring(w, step, c).wait_send()
+
         for w in range(2):
-            side(w, step, core).wait_send()
-            side(w, step, 1 - core).wait_recv()
             late(w, step, core).wait_send()
             late(w, step, 1 - core).wait_recv()
-
-            @pl.when(step < chips - 1)
-            def _():
-                ring(w, step).wait_send()
 
             @pl.when(step > 0)
             def _():
@@ -374,7 +414,7 @@
         out_shape=[jax.ShapeDtypeStruct((peers, depth, kvw), jnp.bfloat16)] * 2,
         in_specs=[hbm] * 2,
         out_specs=[hbm] * 2,
-        scratch_shapes=[pltpu.SemaphoreType.DMA((2,))] + [pltpu.SemaphoreType.DMA((2, chips))] * 8,
+        scratch_shapes=[pltpu.SemaphoreType.DMA((2,))] + [pltpu.SemaphoreType.DMA((2, 2 * chips))] * 8,
         compiler_params=pltpu.CompilerParams(
             collective_id=0, has_side_effects=True, vmem_limit_bytes=LIMIT
         ),
@@ -431,9 +471,8 @@
     prompt_keys, prompt_values = project(
         prompt_states.reshape(pairs_dev * prompt_len, width), key_full, value_full, key_gain
     )
-    out = combine(
-        fetch_index, query_own, prompt_keys, prompt_values, mixed_in, prompt_len, head_dim
-    )
+    own_numer, own_total = prompt_attention(query_own, prompt_keys, prompt_values, prompt_len, head_dim)
+    out = combine(fetch_index, own_numer, own_total, mixed_in, prompt_len, head_dim)
     return out.reshape(queries.shape)
 
 

time: 206 us -> 195 us (0.947)
  Pallas kernels: 131 us -> 127 us
  starting transfers between devices: 15 us -> 11.1 us
  waiting for transfers between devices: 43.3 us -> 39.5 us
    all_to_all x1, starting transfers between devices: 8.35 us -> 4.46 us  [per_device(): lax.all_to_all(mixed, 'pair', split_axis=0, concat_axis=0, tiled=True)]
    all_to_all x1, waiting for transfers between devices: 43.3 us -> 39.5 us  [per_device(): lax.all_to_all(mixed, 'pair', split_axis=0, concat_axis=0, tiled=True)]
    pallas_call x1 -> x2, Pallas kernels: 12 us -> 8.67 us  [the longest x1 4.74 us: combine(): pl.pallas_call(functools.partial(combine_kernel, per, plen, hd), grid_spe...]
    unnamed x31 -> x29, local copies, waits for them, and re-layouts: 13 us -> 13.9 us
  transfers between devices with their start and end apart: 2 -> 2, of which waited for: 1 -> 1; matrix products, arithmetic and copies ran while one was open for 0% -> 0% of each run, Pallas kernels for 53% -> 57%
where the time goes in v4:
time: 195 us; the launch traced here: 194 us
  Pallas kernels  127 us (65%)
  waiting for transfers between devices  39.5 us (20%)
  local copies, waits for them, and re-layouts  14.4 us (7%)
  starting transfers between devices  11.1 us (6%)
  other arithmetic  2.17 us (1%)
    pallas_call x1, Pallas kernels, gather_weights(): pl.pallas_call(functools.partial(ring_kernel, chips, seg), out_shape=[jax...  91.2 us
    all_to_all x1, waiting for transfers between devices, per_device(): lax.all_to_all(mixed, 'pair', split_axis=0, concat_axis=0, tiled=True)  39.5 us
    pallas_call x2, Pallas kernels, project(): pl.pallas_call(functools.partial(project_kernel, hd), grid=(rows // block...  16.1 us
    unnamed x29, local copies, waits for them, and re-layouts  13.9 us
    pallas_call x1, Pallas kernels, owner_attention(): pl.pallas_call(functools.partial(owner_kernel, per, kvw // hd, hd, hd **...  9.7 us
    all_to_all x1, starting transfers between devices, per_device(): lax.all_to_all(outgoing, 'pair', split_axis=0, concat_axis=0, tiled=True)  6.69 us
    pallas_call x1, Pallas kernels, combine(): pl.pallas_call(functools.partial(combine_kernel, per, plen, hd), grid_spe...  4.74 us
    all_to_all x1, starting transfers between devices, per_device(): lax.all_to_all(mixed, 'pair', split_axis=0, concat_axis=0, tiled=True)  4.46 us
  transfers between devices with their start and end apart: 2, of which 1 were waited for; matrix products, arithmetic and copies ran while one was open for 0% of the time, Pallas kernels for 57%

profile of v4, /device:TPU:13, one launch (start us, length us, event | category | flops | bytes accessed | tf_op | source)
XLA Modules:
  0.0 194.5 jit_solution(3477651545113229709)
XLA Ops:
  0.0 0.8 copy.12
  0.8 0.1 eq.34
  0.9 1.4 select_reduce_fusion
  2.4 0.5 convert_reduce_fusion
  2.8 0.1 select_reduce_fusion.4.idx_ref
  3.0 0.0 copy-start.5
  3.0 1.2 copy-done.5
  4.2 0.0 copy-start.13
  4.2 0.7 copy-done.13
  4.8 1.5 shard_map.100
  6.3 0.0 copy-start.1
  6.3 1.3 copy-done.1
  7.6 0.0 copy-start.10
  7.6 0.0 copy-start.12
  7.6 6.7 %all-to-all-start = ((bf16[32,256,128]{2,1,0:T(8,128)(2,1)}), bf16[32,256,128]{2,1,0:T(8,128)(2,1)S(1)}, u32[]{:S(2)}, u32[]{:S(2)}) async-start(bf16[32,256,128]{2,1,0:T(8,128)(2,1)} %copy-done.1), calls=%async_computation | async-start | bytes 4194304 | tf_op jit(solution)/shard_map/all_to_all | solution.py:457
  14.3 0.1 select_reduce_fusion.2
  14.5 0.1 copy.14
  14.6 0.1 max.7.len_ref
  14.7 0.1 copy.13
  14.8 0.1 reshape.148.slot_ref
  14.9 0.0 copy-done.10
  14.9 0.0 copy-start.11
  14.9 1.0 copy-done.11
  15.8 91.2 %shard_map.101 = (bf16[16,320,512]{2,1,0:T(8,128)(2,1)S(1)}, bf16[16,320,512]{2,1,0:T(8,128)(2,1)}) custom-call(bf16[320,512]{1,0:T(8,128)(2,1)S(1)} %copy-done.10, bf16[320,512]{1,0:T(8,128)(2,1)S(1)} %copy-done.11), custom_call_target="tpu_custom_call" | custom-call | tf_op jit(solution)/shard_map/pallas_call | solution.py:412
  107.0 0.0 copy-start
  107.0 2.3 %copy-done = bf16[16,320,512]{2,1,0:T(8,128)(2,1)} copy-done((bf16[16,320,512]{2,1,0:T(8,128)(2,1)}, bf16[16,320,512]{2,1,0:T(8,128)(2,1)S(1)}, u32[]{:S(2)}) %copy-start) | copy-done | bytes 5242904
  109.4 0.0 copy-done.12
  109.4 10.6 %shard_map.104 = (bf16[512,512]{1,0:T(8,128)(2,1)S(1)}, bf16[512,512]{1,0:T(8,128)(2,1)S(1)}) custom-call(bf16[512,5120]{1,0:T(8,128)(2,1)} %bitcast.23, bf16[5120,512]{1,0:T(8,128)(2,1)} %bitcast.12, bf16[5120,512]{1,0:T(8,128)(2,1)} %bitcast.21, f32[1,128]{1,0:T(1,128)S(1)} %bitcast.18), custom_call_target="tpu_custom_call" | custom-call | tf_op jit(solution)/shard_map/pallas_call | solution.py:86
  119.9 0.0 copy-start.6
  119.9 0.8 copy-done.6
  120.7 0.0 copy-start.8
  120.7 0.8 copy-done.8
  121.5 0.0 all-to-all-done.q_ref
  121.5 0.0 copy-start.7
  121.6 1.0 copy-done.7
  122.6 0.0 copy-start.9
  122.6 1.0 copy-done.9
  123.6 9.7 %shard_map.105 = bf16[32,272,128]{2,1,0:T(8,128)(2,1)} custom-call(s32[32]{0:T(128)S(1)} %reshape.148.slot_ref, s32[32]{0:T(128)S(1)} %max.7.len_ref, bf16[32,256,128]{2,1,0:T(8,128)(2,1)S(1)} %all-to-all-done.q_ref, bf16[4,128,512]{2,1,0:T(8,128)(2,1)S(1)} %bitcast.16, bf16[4,128,512]{2,1,0:T(8,128)(2,1)S(1)} %bitcast.17), custom_call_target="tpu_custom_call" | custom-call | tf_op jit(solution)/shard_map/pallas_call | solution.py:168
  133.3 0.0 copy-start.4
  133.3 4.5 %all-to-all-start.1 = ((bf16[32,272,128]{2,1,0:T(8,128)(2,1)}), bf16[32,272,128]{2,1,0:T(8,128)(2,1)}, u32[]{:S(2)}, u32[]{:S(2)}) async-start(bf16[32,272,128]{2,1,0:T(8,128)(2,1)} %shard_map.105), calls=%async_computation.1 | async-start | bytes 4456448 | tf_op jit(solution)/shard_map/all_to_all | solution.py:470
  137.8 0.0 copy-done.4
  137.8 5.6 %shard_map.102 = (bf16[128,512]{1,0:T(8,128)(2,1)S(1)}, bf16[128,512]{1,0:T(8,128)(2,1)S(1)}) custom-call(bf16[128,5120]{1,0:T(8,128)(2,1)S(1)} %bitcast.14, bf16[5120,512]{1,0:T(8,128)(2,1)} %bitcast.13, bf16[5120,512]{1,0:T(8,128)(2,1)} %bitcast.22, f32[1,128]{1,0:T(1,128)S(1)} %bitcast.19), custom_call_target="tpu_custom_call" | custom-call | tf_op jit(solution)/shard_map/pallas_call | solution.py:86
  143.4 3.9 %shard_map.103 = (f32[16,256,128]{2,1,0:T(8,128)S(1)}, f32[16,256,128]{2,1,0:T(8,128)S(1)}) custom-call(bf16[16,256,128]{2,1,0:T(8,128)(2,1)S(1)} %get-tuple-element.15.q_ref, bf16[128,512]{1,0:T(8,128)(2,1)S(1)} %get-tuple-element.18.k_ref, bf16[128,512]{1,0:T(8,128)(2,1)S(1)} %get-tuple-element.19.v_ref), custom_call_target="tpu_custom_call" | custom-call | tf_op jit(solution)/shard_map/pallas_call | solution.py:224
  147.3 0.0 copy-start.2
  147.4 1.3 copy-done.2
  148.7 39.5 %all-to-all-done.1.in_ref = bf16[32,272,128]{2,1,0:T(8,128)(2,1)} async-done(((bf16[32,272,128]{2,1,0:T(8,128)(2,1)}), bf16[32,272,128]{2,1,0:T(8,128)(2,1)}, u32[]{:S(2)}, u32[]{:S(2)}) %all-to-all-start.1) | async-done | bytes 2228256 | tf_op jit(solution)/shard_map/all_to_all | solution.py:470
  188.2 0.0 copy-start.3
  188.2 1.6 copy-done.3
  189.7 4.7 %shard_map.106 = bf16[128,4096]{1,0:T(8,128)(2,1)} custom-call(s32[32]{0:T(128)S(1)} %add_bitcast_fusion.at_ref, f32[16,256,128]{2,1,0:T(8,128)S(1)} %get-tuple-element.20.n_ref, f32[16,256,128]{2,1,0:T(8,128)S(1)} %copy-done.3, bf16[32,272,128]{2,1,0:T(8,128)(2,1)} %all-to-all-done.1.in_ref), custom_call_target="tpu_custom_call" | custom-call | tf_op jit(solution)/shard_map/pallas_call | solution.py:257
  (6 shorter events, 0.1 us)
Async XLA Ops:
  3.0 1.2 copy-start.5
  4.2 0.7 copy-start.13
  6.3 1.3 copy-start.1
  7.6 7.2 %copy-start.10 = (bf16[320,512]{1,0:T(8,128)(2,1)S(1)}, bf16[320,512]{1,0:T(8,128)(2,1)}, u32[]{:S(2)}) copy-start(bf16[320,512]{1,0:T(8,128)(2,1)} %wk_ref.1) | copy-start | bytes 983044
  7.6 101.7 %copy-start.12 = (f32[128]{0:T(128)S(1)}, f32[128]{0:T(128)}, u32[]{:S(2)}) copy-start(f32[128]{0:T(128)} %param.15) | copy-start | bytes 1540
  7.6 113.9 %all-to-all-start = ((bf16[32,256,128]{2,1,0:T(8,128)(2,1)}), bf16[32,256,128]{2,1,0:T(8,128)(2,1)S(1)}, u32[]{:S(2)}, u32[]{:S(2)}) async-start(bf16[32,256,128]{2,1,0:T(8,128)(2,1)} %copy-done.1), calls=%async_computation | async-start | bytes 4194304 | tf_op jit(solution)/shard_map/all_to_all | solution.py:457
  14.9 1.0 copy-start.11
  107.0 2.3 %copy-start = (bf16[16,320,512]{2,1,0:T(8,128)(2,1)}, bf16[16,320,512]{2,1,0:T(8,128)(2,1)S(1)}, u32[]{:S(2)}) copy-start(bf16[16,320,512]{2,1,0:T(8,128)(2,1)S(1)} %get-tuple-element.16) | copy-start | bytes 15728644
  119.9 0.8 copy-start.6
  120.7 0.8 copy-start.8
  121.5 1.0 copy-start.7
  122.6 1.0 copy-start.9
  133.3 4.5 %copy-start.4 = (bf16[16,8,5120]{2,1,0:T(8,128)(2,1)S(1)}, bf16[16,8,5120]{2,1,0:T(8,128)(2,1)}, u32[]{:S(2)}) copy-start(bf16[16,8,5120]{2,1,0:T(8,128)(2,1)} %param.11) | copy-start | bytes 3932164
  133.3 54.8 %all-to-all-start.1 = ((bf16[32,272,128]{2,1,0:T(8,128)(2,1)}), bf16[32,272,128]{2,1,0:T(8,128)(2,1)}, u32[]{:S(2)}, u32[]{:S(2)}) async-start(bf16[32,272,128]{2,1,0:T(8,128)(2,1)} %shard_map.105), calls=%async_computation.1 | async-start | bytes 4456448 | tf_op jit(solution)/shard_map/all_to_all | solution.py:470
  147.3 1.3 copy-start.2
  188.2 1.6 copy-start.3

commit v5 on v4

--- a/solution.py
+++ b/solution.py
@@ -9,7 +9,6 @@
 norm_eps = 1e-06
 VMEM = pltpu.VMEM
 LIMIT = 48 * 1024 * 1024
-USE_RING = True
 
 
 def table_lookup(table, indices):
@@ -268,8 +267,9 @@
 
 
 def ring_kernel(
-    chips, seg, wk_ref, wv_ref, ok_ref, ov_ref,
-    own_sem, ring_send, ring_recv, side_send, side_recv, swap_send, swap_recv, late_send, late_recv,
+    chips, seg, hd, wk_ref, wv_ref, xa_ref, xp_ref, gain_ref, ak_ref, av_ref, pk_ref, pv_ref,
+    keys_buf, values_buf, x_buf, key_acc, value_acc, own_sem, x_sem,
+    ring_send, ring_recv, side_send, side_recv, swap_send, swap_recv, late_send, late_recv,
 ):
     me = lax.axis_index("pair")
     group = lax.axis_index("groups")
@@ -295,25 +295,34 @@
     for other in (right, left, sibling, twin):
         pl.semaphore_signal(barrier, inc=1, device_id=other, device_id_type=mesh_id)
     own = []
-    outs = (ok_ref, ov_ref)
-    for w, (src, out) in enumerate(((wk_ref, ok_ref), (wv_ref, ov_ref))):
-        copy = pltpu.make_async_copy(src, out.at[me], own_sem.at[w])
+    outs = (keys_buf, values_buf)
+    accs = (key_acc, value_acc)
+    for w, (src, out) in enumerate(((wk_ref, keys_buf), (wv_ref, values_buf))):
+        place = pl.ds(pl.multiple_of(core * depth, 16), depth)
+        copy = pltpu.make_async_copy(src, out.at[chip, place], own_sem.at[w])
         copy.start()
         own.append(copy)
+    answers = xa_ref.shape[0]
+    total_rows = x_buf.shape[0]
+    x_copies = (
+        pltpu.make_async_copy(xa_ref, x_buf.at[:answers], x_sem.at[0]),
+        pltpu.make_async_copy(xp_ref, x_buf.at[answers:], x_sem.at[1]),
+    )
+    for copy in x_copies:
+        copy.start()
     for copy in own:
         copy.wait()
     pl.semaphore_wait(barrier, 4)
 
     first = ((depth - seg) // 16 + 1) // 2 * 16
-    chunks = tuple(
-        pl.ds(pl.multiple_of(odd_group * seg + start, 16), size)
-        for start, size in ((0, first), (first, depth - seg - first))
-    )
-    mine = pl.ds(pl.multiple_of(odd_group * (depth - seg), 16), seg)
-    other_rows = pl.ds(pl.multiple_of((1 - odd_group) * (depth - seg), 16), seg)
-
-    def piece(w, step, on):
-        return chip_at(position - step if w == 0 else position + step) * 2 + on
+    pieces = ((odd_group * seg, first), (odd_group * seg + first, depth - seg - first))
+    mine = (odd_group * (depth - seg), seg)
+    other_rows = ((1 - odd_group) * (depth - seg), seg)
+
+    def block_of(w, step, on, rows):
+        at = chip_at(position - step if w == 0 else position + step)
+        start, size = rows
+        return outs[w].at[at, pl.ds(pl.multiple_of(on * depth + start, 16), size)]
 
     def remote(block, send, recv, target):
         return pltpu.make_async_remote_copy(
@@ -321,21 +330,21 @@
         )
 
     def ring(w, step, c, arriving=0):
-        block = outs[w].at[piece(w, step + arriving, core), chunks[c]]
+        block = block_of(w, step + arriving, core, pieces[c])
         at = 2 * step + c
         return remote(block, ring_send.at[w, at], ring_recv.at[w, at], partners[w])
 
     def side(w, step, c, on):
-        block = outs[w].at[piece(w, step, on), chunks[c]]
+        block = block_of(w, step, on, pieces[c])
         at = 2 * step + c
         return remote(block, side_send.at[w, at], side_recv.at[w, at], sibling)
 
     def swap(w, step, rows):
-        block = outs[w].at[piece(w, step, core), rows]
+        block = block_of(w, step, core, rows)
         return remote(block, swap_send.at[w, step], swap_recv.at[w, step], twin)
 
     def late(w, step, on):
-        block = outs[w].at[piece(w, step, on), other_rows]
+        block = block_of(w, step, on, other_rows)
         return remote(block, late_send.at[w, step], late_recv.at[w, step], sibling)
 
     both = [(c, w) for c in range(2) for w in range(2)]
@@ -351,7 +360,29 @@
             swap(w, step, other_rows).wait_recv()
             late(w, step, core).start()
 
-    lag = 3
+    lag = 2
+    for copy in x_copies:
+        copy.wait()
+    for acc in accs:
+        acc[...] = jnp.zeros_like(acc)
+    half = total_rows // 2
+
+    def multiply(step):
+        for w in range(2):
+            for c in range(2):
+                side(w, step, c, 1 - core).wait_recv()
+            late(w, step, 1 - core).wait_recv()
+            at = chip_at(position - step if w == 0 else position + step)
+            cols = pl.ds(pl.multiple_of(at * 2 * depth, 128), 2 * depth)
+
+            def part(i, carry):
+                rows = pl.ds(pl.multiple_of(i * half, 16), half)
+                accs[w][rows, :] += jnp.dot(
+                    x_buf[rows, cols], outs[w][at], preferred_element_type=jnp.float32
+                )
+                return carry
+
+            lax.fori_loop(0, 2, part, 0)
 
     def body(step, carry):
         for c, w in both:
@@ -369,6 +400,10 @@
         def _():
             hand_over(step - lag)
 
+        @pl.when(step > lag)
+        def _():
+            multiply(step - lag - 1)
+
         return carry
 
     lax.fori_loop(1, chips, body, 0)
@@ -379,10 +414,26 @@
 
     lax.fori_loop(chips - lag, chips, finish, 0)
 
+    def rest(step, carry):
+        multiply(step)
+        return carry
+
+    lax.fori_loop(chips - lag - 1, chips, rest, 0)
+
+    block = 128
+    for i in range(total_rows // block):
+        rows = slice(i * block, (i + 1) * block)
+        inside = i * block < answers
+        to_k, to_v = (ak_ref, av_ref) if inside else (pk_ref, pv_ref)
+        to = slice(i * block - (0 if inside else answers), (i + 1) * block - (0 if inside else answers))
+        for h in range(key_acc.shape[1] // hd):
+            cols = slice(h * hd, (h + 1) * hd)
+            to_k[to, cols] = norm_rows(key_acc[rows, cols], gain_ref[...]).astype(jnp.bfloat16)
+        to_v[to, :] = value_acc[rows, :].astype(jnp.bfloat16)
+
     def drain(step, carry):
         for c, w in both:
             side(w, step, c, core).wait_send()
-            side(w, step, c, 1 - core).wait_recv()
 
             @pl.when(step < chips - 1)
             def _():
@@ -390,7 +441,6 @@
 
         for w in range(2):
             late(w, step, core).wait_send()
-            late(w, step, 1 - core).wait_recv()
 
             @pl.when(step > 0)
             def _():
@@ -401,25 +451,37 @@
     lax.fori_loop(0, chips, drain, 0)
 
 
-def gather_weights(w_key, w_value):
+def encode(w_key, w_value, answer_x, prompt_x, gain):
     peers = lax.axis_size("pair")
     depth, kvw = w_key.shape
-    if not USE_RING:
-        return tuple(lax.all_gather(w, "pair", axis=0, tiled=True) for w in (w_key, w_value))
+    hd = gain.shape[0]
+    if 2 * depth % 128:
+        key_full, value_full = (lax.all_gather(w, "pair", axis=0, tiled=True) for w in (w_key, w_value))
+        return (
+            *project(answer_x, key_full, value_full, gain),
+            *project(prompt_x, key_full, value_full, gain),
+        )
     chips = peers // 2
     seg = max(1, round(depth // 16 * 0.35)) * 16
-    hbm = pl.BlockSpec(memory_space=pl.ANY)
-    out = pl.pallas_call(
-        functools.partial(ring_kernel, chips, seg),
-        out_shape=[jax.ShapeDtypeStruct((peers, depth, kvw), jnp.bfloat16)] * 2,
-        in_specs=[hbm] * 2,
-        out_specs=[hbm] * 2,
-        scratch_shapes=[pltpu.SemaphoreType.DMA((2,))] + [pltpu.SemaphoreType.DMA((2, 2 * chips))] * 8,
+    answers, width = answer_x.shape
+    prompts = prompt_x.shape[0]
+    anywhere = pl.BlockSpec(memory_space=pl.ANY)
+    vmem = pl.BlockSpec(memory_space=VMEM)
+    dma = pltpu.SemaphoreType.DMA
+    return pl.pallas_call(
+        functools.partial(ring_kernel, chips, seg, hd),
+        out_shape=[jax.ShapeDtypeStruct((n, kvw), jnp.bfloat16) for n in (answers, answers, prompts, prompts)],
+        in_specs=[anywhere] * 4 + [vmem],
+        out_specs=[vmem] * 4,
+        scratch_shapes=[VMEM((chips, 2 * depth, kvw), jnp.bfloat16)] * 2
+        + [VMEM((answers + prompts, width), jnp.bfloat16)]
+        + [VMEM((answers + prompts, kvw), jnp.float32)] * 2
+        + [dma((2,))] * 2
+        + [dma((2, 2 * chips))] * 8,
         compiler_params=pltpu.CompilerParams(
             collective_id=0, has_side_effects=True, vmem_limit_bytes=LIMIT
         ),
-    )(w_key, w_value)
-    return tuple(w.reshape(peers * depth, kvw) for w in out)
+    )(w_key, w_value, answer_x, prompt_x, gain.reshape(1, hd))
 
 
 def per_device(
@@ -455,9 +517,12 @@
 
     query_own, outgoing = prepare_queries(ref_pair, queries, query_gain)
     asked = lax.all_to_all(outgoing, "pair", split_axis=0, concat_axis=0, tiled=True)
-    key_full, value_full = gather_weights(w_key, w_value)
-    answer_keys, answer_values = project(
-        answer_states.reshape(ans_dev * ans_len, width), key_full, value_full, key_gain
+    answer_keys, answer_values, prompt_keys, prompt_values = encode(
+        w_key,
+        w_value,
+        answer_states.reshape(ans_dev * ans_len, width),
+        prompt_states.reshape(pairs_dev * prompt_len, width),
+        key_gain,
     )
     mixed = owner_attention(
         slot_local,
@@ -468,9 +533,6 @@
         head_dim,
     )
     mixed_in = lax.all_to_all(mixed, "pair", split_axis=0, concat_axis=0, tiled=True)
-    prompt_keys, prompt_values = project(
-        prompt_states.reshape(pairs_dev * prompt_len, width), key_full, value_full, key_gain
-    )
     own_numer, own_total = prompt_attention(query_own, prompt_keys, prompt_values, prompt_len, head_dim)
     out = combine(fetch_index, own_numer, own_total, mixed_in, prompt_len, head_dim)
     return out.reshape(queries.shape)

time: 195 us -> 188 us (0.964)
  Pallas kernels: 127 us -> 113 us
  waiting for transfers between devices: 39.5 us -> 45 us
    pallas_call x3 -> x1, Pallas kernels: 107 us -> 93.3 us  [encode(): pl.pallas_call(functools.partial(ring_kernel, chips, seg, hd), out_shape=...]
    all_to_all x1, waiting for transfers between devices: 39.5 us -> 45 us  [per_device(): lax.all_to_all(mixed, 'pair', split_axis=0, concat_axis=0, tiled=True)]
    unnamed x29 -> x35, local copies, waits for them, and re-layouts: 13.9 us -> 14.2 us
  transfers between devices with their start and end apart: 2 -> 2, of which waited for: 1 -> 1; matrix products, arithmetic and copies ran while one was open for 0% -> 0% of each run, Pallas kernels for 57% -> 52%
where the time goes in v5:
time: 188 us; the launch traced here: 187 us
  Pallas kernels  113 us (60%)
  waiting for transfers between devices  45 us (24%)
  local copies, waits for them, and re-layouts  14.7 us (8%)
  starting transfers between devices  12.1 us (6%)
  other arithmetic  2.17 us (1%)
    pallas_call x1, Pallas kernels, encode(): pl.pallas_call(functools.partial(ring_kernel, chips, seg, hd), out_shape=...  93.3 us
    all_to_all x1, waiting for transfers between devices, per_device(): lax.all_to_all(mixed, 'pair', split_axis=0, concat_axis=0, tiled=True)  45 us
    unnamed x35, local copies, waits for them, and re-layouts  14.2 us
    pallas_call x1, Pallas kernels, owner_attention(): pl.pallas_call(functools.partial(owner_kernel, per, kvw // hd, hd, hd **...  9.68 us
    all_to_all x1, starting transfers between devices, per_device(): lax.all_to_all(outgoing, 'pair', split_axis=0, concat_axis=0, tiled=True)  6.69 us
    all_to_all x1, starting transfers between devices, per_device(): lax.all_to_all(mixed, 'pair', split_axis=0, concat_axis=0, tiled=True)  5.38 us
    pallas_call x1, Pallas kernels, combine(): pl.pallas_call(functools.partial(combine_kernel, per, plen, hd), grid_spe...  4.74 us
    pallas_call x1, Pallas kernels, prompt_attention(): pl.pallas_call(functools.partial(prompt_kernel, per, plen, kvw // hd, hd,...  3.94 us
  transfers between devices with their start and end apart: 2, of which 1 were waited for; matrix products, arithmetic and copies ran while one was open for 0% of the time, Pallas kernels for 52%

profile of v5, /device:TPU:13, one launch (start us, length us, event | category | flops | bytes accessed | tf_op | source)
XLA Modules:
  0.0 187.2 jit_solution(11325048071938811579)
XLA Ops:
  0.0 0.8 copy.12
  0.8 0.1 eq.34
  0.9 1.4 select_reduce_fusion
  2.4 0.5 convert_reduce_fusion
  2.8 0.1 select_reduce_fusion.4.idx_ref
  3.0 0.0 copy-start.6
  3.0 1.2 copy-done.6
  4.2 0.0 copy-start.15
  4.2 0.7 copy-done.15
  4.8 1.4 shard_map.100
  6.3 0.0 copy-start
  6.3 1.3 copy-done
  7.6 0.0 copy-start.4
  7.6 1.0 copy-done.4
  8.6 0.0 copy-start.3
  8.6 0.0 copy-start.16
  8.6 6.7 %all-to-all-start = ((bf16[32,256,128]{2,1,0:T(8,128)(2,1)}), bf16[32,256,128]{2,1,0:T(8,128)(2,1)S(1)}, u32[]{:S(2)}, u32[]{:S(2)}) async-start(bf16[32,256,128]{2,1,0:T(8,128)(2,1)} %copy-done), calls=%async_computation | async-start | bytes 4194304 | tf_op jit(solution)/shard_map/all_to_all | solution.py:519
  15.3 0.1 select_reduce_fusion.2
  15.5 0.1 copy.14
  15.6 0.1 max.7.len_ref
  15.7 0.1 copy.13
  15.7 0.1 reshape.140.slot_ref
  15.8 0.0 copy-done.3
  15.8 0.0 copy-done.16
  15.8 0.0 copy-start.11
  15.9 1.0 copy-done.11
  16.8 0.0 copy-start.12
  16.8 1.0 copy-done.12
  17.8 93.3 %shard_map.101 = (bf16[512,512]{1,0:T(8,128)(2,1)S(1)}, bf16[512,512]{1,0:T(8,128)(2,1)S(1)}, bf16[128,512]{1,0:T(8,128)(2,1)S(1)}, bf16[128,512]{1,0:T(8,128)(2,1)S(1)}) custom-call(bf16[320,512]{1,0:T(8,128)(2,1)S(1)} %copy-done.11, bf16[320,512]{1,0:T(8,128)(2,1)S(1)} %copy-done.12, bf16[512,5120]{1,0:T(8,128)(2,1)} %bitcast.16, ...), custom_call_target="tpu_custom_call" | custom-call | tf_op jit(solution)/shard_map/pallas_call | solution.py:471
  111.1 0.0 copy-start.7
  111.1 0.8 copy-done.7
  111.9 0.0 copy-start.9
  111.9 0.8 copy-done.9
  112.7 0.0 copy-start.13
  112.7 0.7 copy-done.13
  113.4 0.0 all-to-all-done.q_ref
  113.4 0.0 copy-start.8
  113.4 1.0 copy-done.8
  114.4 0.0 copy-start.10
  114.4 1.0 copy-done.10
  115.5 9.7 %shard_map.103 = bf16[32,272,128]{2,1,0:T(8,128)(2,1)} custom-call(s32[32]{0:T(128)S(1)} %reshape.140.slot_ref, s32[32]{0:T(128)S(1)} %max.7.len_ref, bf16[32,256,128]{2,1,0:T(8,128)(2,1)S(1)} %all-to-all-done.q_ref, bf16[4,128,512]{2,1,0:T(8,128)(2,1)S(1)} %bitcast.12, bf16[4,128,512]{2,1,0:T(8,128)(2,1)S(1)} %bitcast.13), custom_call_target="tpu_custom_call" | custom-call | tf_op jit(solution)/shard_map/pallas_call | solution.py:167
  125.1 0.0 copy-start.5
  125.1 0.0 copy-start.14
  125.1 5.4 %all-to-all-start.1 = ((bf16[32,272,128]{2,1,0:T(8,128)(2,1)}), bf16[32,272,128]{2,1,0:T(8,128)(2,1)}, u32[]{:S(2)}, u32[]{:S(2)}) async-start(bf16[32,272,128]{2,1,0:T(8,128)(2,1)} %shard_map.103), calls=%async_computation.1 | async-start | bytes 4456448 | tf_op jit(solution)/shard_map/all_to_all | solution.py:535
  130.5 0.0 copy-done.5
  130.5 0.0 copy-done.14
  130.5 3.9 %shard_map.102 = (f32[16,256,128]{2,1,0:T(8,128)S(1)}, f32[16,256,128]{2,1,0:T(8,128)S(1)}) custom-call(bf16[16,256,128]{2,1,0:T(8,128)(2,1)S(1)} %copy-done.5, bf16[128,512]{1,0:T(8,128)(2,1)S(1)} %get-tuple-element.14.k_ref, bf16[128,512]{1,0:T(8,128)(2,1)S(1)} %copy-done.14), custom_call_target="tpu_custom_call" | custom-call | tf_op jit(solution)/shard_map/pallas_call | solution.py:223
  134.5 0.0 copy-start.1
  134.5 1.3 copy-done.1
  135.8 45.0 %all-to-all-done.1.in_ref = bf16[32,272,128]{2,1,0:T(8,128)(2,1)} async-done(((bf16[32,272,128]{2,1,0:T(8,128)(2,1)}), bf16[32,272,128]{2,1,0:T(8,128)(2,1)}, u32[]{:S(2)}, u32[]{:S(2)}) %all-to-all-start.1) | async-done | bytes 2228256 | tf_op jit(solution)/shard_map/all_to_all | solution.py:535
  180.9 0.0 copy-start.2
  180.9 1.6 copy-done.2
  182.4 4.7 %shard_map.104 = bf16[128,4096]{1,0:T(8,128)(2,1)} custom-call(s32[32]{0:T(128)S(1)} %add_bitcast_fusion.at_ref, f32[16,256,128]{2,1,0:T(8,128)S(1)} %get-tuple-element.16.n_ref, f32[16,256,128]{2,1,0:T(8,128)S(1)} %copy-done.2, bf16[32,272,128]{2,1,0:T(8,128)(2,1)} %all-to-all-done.1.in_ref), custom_call_target="tpu_custom_call" | custom-call | tf_op jit(solution)/shard_map/pallas_call | solution.py:256
  (6 shorter events, 0.1 us)
Async XLA Ops:
  3.0 1.2 copy-start.6
  4.2 0.7 copy-start.15
  6.3 1.3 copy-start
  7.6 1.0 copy-start.4
  8.6 7.2 %copy-start.3 = (bf16[16,8,5120]{2,1,0:T(8,128)(2,1)S(1)}, bf16[16,8,5120]{2,1,0:T(8,128)(2,1)}, u32[]{:S(2)}) copy-start(bf16[16,8,5120]{2,1,0:T(8,128)(2,1)} %param.11) | copy-start | bytes 3932164
  8.6 7.2 %copy-start.16 = (f32[128]{0:T(128)S(1)}, f32[128]{0:T(128)}, u32[]{:S(2)}) copy-start(f32[128]{0:T(128)} %param.15) | copy-start | bytes 1540
  8.6 104.7 %all-to-all-start = ((bf16[32,256,128]{2,1,0:T(8,128)(2,1)}), bf16[32,256,128]{2,1,0:T(8,128)(2,1)S(1)}, u32[]{:S(2)}, u32[]{:S(2)}) async-start(bf16[32,256,128]{2,1,0:T(8,128)(2,1)} %copy-done), calls=%async_computation | async-start | bytes 4194304 | tf_op jit(solution)/shard_map/all_to_all | solution.py:519
  15.8 1.0 copy-start.11
  16.8 1.0 copy-start.12
  111.1 0.8 copy-start.7
  111.9 0.8 copy-start.9
  112.7 0.7 copy-start.13
  113.4 1.0 copy-start.8
  114.4 1.0 copy-start.10
  125.1 5.4 %copy-start.5 = (bf16[16,256,128]{2,1,0:T(8,128)(2,1)S(1)}, bf16[16,256,128]{2,1,0:T(8,128)(2,1)}, u32[]{:S(2)}) copy-start(bf16[16,256,128]{2,1,0:T(8,128)(2,1)} %copy-done.4) | copy-start | bytes 3145732
  125.1 5.4 %copy-start.14 = (bf16[128,512]{1,0:T(8,128)(2,1)S(1)}, bf16[128,512]{1,0:T(8,128)(2,1)}, u32[]{:S(2)}) copy-start(bf16[128,512]{1,0:T(8,128)(2,1)} %copy-done.13) | copy-start | bytes 393220
  125.1 55.7 %all-to-all-start.1 = ((bf16[32,272,128]{2,1,0:T(8,128)(2,1)}), bf16[32,272,128]{2,1,0:T(8,128)(2,1)}, u32[]{:S(2)}, u32[]{:S(2)}) async-start(bf16[32,272,128]{2,1,0:T(8,128)(2,1)} %shard_map.103), calls=%async_computation.1 | async-start | bytes 4456448 | tf_op jit(solution)/shard_map/all_to_all | solution.py:535
  134.5 1.3 copy-start.1
  180.9 1.6 copy-start.2

commit v6 on v5

--- a/solution.py
+++ b/solution.py
@@ -8,7 +8,7 @@
 
 norm_eps = 1e-06
 VMEM = pltpu.VMEM
-LIMIT = 48 * 1024 * 1024
+LIMIT = 60 * 1024 * 1024
 
 
 def table_lookup(table, indices):
@@ -462,7 +462,7 @@
             *project(prompt_x, key_full, value_full, gain),
         )
     chips = peers // 2
-    seg = max(1, round(depth // 16 * 0.35)) * 16
+    seg = max(1, round(depth // 16 * 0.45)) * 16
     answers, width = answer_x.shape
     prompts = prompt_x.shape[0]
     anywhere = pl.BlockSpec(memory_space=pl.ANY)

time: 188 us -> 196 us (1.043)
  Pallas kernels: 113 us -> 131 us
  local copies, waits for them, and re-layouts: 14.7 us -> 5.08 us
    unnamed x35 -> x7, local copies, waits for them, and re-layouts: 14.2 us -> 3.5 us
    pallas_call x1, Pallas kernels: 93.3 us -> 104 us  [encode(): pl.pallas_call(functools.partial(ring_kernel, chips, seg, hd), out_shape=...]
    pallas_call x1, Pallas kernels: 1.45 us -> 3.85 us  [prepare_queries(): pl.pallas_call(functools.partial(query_kernel, pairs, plen, heads, hd, sl...]
    pallas_call x1, Pallas kernels: 3.94 us -> 6.15 us  [prompt_attention(): pl.pallas_call(functools.partial(prompt_kernel, per, plen, kvw // hd, hd,...]
  transfers between devices with their start and end apart: 2 -> 2, of which waited for: 1 -> 1; matrix products, arithmetic and copies ran while one was open for 0% -> 1% of each run, Pallas kernels for 52% -> 56%
where the time goes in v6:
time: 196 us; the launch traced here: 195 us
  Pallas kernels  131 us (67%)
  waiting for transfers between devices  44.1 us (22%)
  starting transfers between devices  12.4 us (6%)
  local copies, waits for them, and re-layouts  5.08 us (3%)
  other arithmetic  2.69 us (1%)
    pallas_call x1, Pallas kernels, encode(): pl.pallas_call(functools.partial(ring_kernel, chips, seg, hd), out_shape=...  104 us
    all_to_all x1, waiting for transfers between devices, per_device(): lax.all_to_all(mixed, 'pair', split_axis=0, concat_axis=0, tiled=True)  44.1 us
    pallas_call x1, Pallas kernels, owner_attention(): pl.pallas_call(functools.partial(owner_kernel, per, kvw // hd, hd, hd **...  11.1 us
    all_to_all x1, starting transfers between devices, per_device(): lax.all_to_all(outgoing, 'pair', split_axis=0, concat_axis=0, tiled=True)  6.56 us
    pallas_call x1, Pallas kernels, prompt_attention(): pl.pallas_call(functools.partial(prompt_kernel, per, plen, kvw // hd, hd,...  6.15 us
    pallas_call x1, Pallas kernels, combine(): pl.pallas_call(functools.partial(combine_kernel, per, plen, hd), grid_spe...  6.07 us
    all_to_all x1, starting transfers between devices, per_device(): lax.all_to_all(mixed, 'pair', split_axis=0, concat_axis=0, tiled=True)  5.84 us
  transfers between devices with their start and end apart: 2, of which 1 were waited for; matrix products, arithmetic and copies ran while one was open for 1% of the time, Pallas kernels for 56%

profile of v6, /device:TPU:13, one launch (start us, length us, event | category | flops | bytes accessed | tf_op | source)
XLA Modules:
  0.0 195.3 jit_solution(985206606494635652)
XLA Ops:
  0.0 0.8 copy.12
  0.8 0.1 eq.34
  0.9 1.4 select_reduce_fusion
  2.4 0.5 convert_reduce_fusion
  2.8 0.0 copy-start.2
  2.9 0.6 select_reduce_fusion.4.idx_ref
  3.5 3.9 %shard_map.100 = (bf16[16,256,128]{2,1,0:T(8,128)(2,1)}, bf16[32,256,128]{2,1,0:T(8,128)(2,1)}) custom-call(s32[32]{0:T(128)} %select_reduce_fusion.4.idx_ref, bf16[128,4096]{1,0:T(8,128)(2,1)} %bitcast.12, f32[1,128]{1,0:T(1,128)} %bitcast.15), custom_call_target="tpu_custom_call" | custom-call | tf_op jit(solution)/shard_map/pallas_call | solution.py:54
  7.3 0.0 copy-done.2
  7.3 6.6 %all-to-all-start = ((bf16[32,256,128]{2,1,0:T(8,128)(2,1)}), bf16[32,256,128]{2,1,0:T(8,128)(2,1)S(1)}, u32[]{:S(2)}, u32[]{:S(2)}) async-start(bf16[32,256,128]{2,1,0:T(8,128)(2,1)} %get-tuple-element.18), calls=%async_computation | async-start | bytes 4194304 | tf_op jit(solution)/shard_map/all_to_all | solution.py:519
  13.9 0.1 select_reduce_fusion.2
  14.1 0.1 copy.14
  14.2 0.7 max.7.len_ref
  14.8 0.1 copy.13
  14.9 0.6 reshape.140.slot_ref
  15.5 103.8 %shard_map.101 = (bf16[512,512]{1,0:T(8,128)(2,1)}, bf16[512,512]{1,0:T(8,128)(2,1)}, bf16[128,512]{1,0:T(8,128)(2,1)}, bf16[128,512]{1,0:T(8,128)(2,1)}) custom-call(bf16[320,512]{1,0:T(8,128)(2,1)} %wk_ref.1, bf16[320,512]{1,0:T(8,128)(2,1)} %wv_ref.1, bf16[512,5120]{1,0:T(8,128)(2,1)} %bitcast.10, bf16[128,5120]{1,0:T(8,128)(2,1)} %bitcast.11, ...), custom_call_target="tpu_custom_call" | custom-call | tf_op jit(solution)/shard_map/pallas_call | solution.py:471
  119.3 0.0 all-to-all-done.q_ref
  119.3 0.0 copy-start.1
  119.3 1.3 copy-done.1
  120.6 11.1 %shard_map.103 = bf16[32,272,128]{2,1,0:T(8,128)(2,1)} custom-call(s32[32]{0:T(128)} %reshape.140.slot_ref, s32[32]{0:T(128)} %max.7.len_ref, bf16[32,256,128]{2,1,0:T(8,128)(2,1)} %copy-done.1, bf16[4,128,512]{2,1,0:T(8,128)(2,1)} %bitcast.13, bf16[4,128,512]{2,1,0:T(8,128)(2,1)} %bitcast.14), custom_call_target="tpu_custom_call" | custom-call | tf_op jit(solution)/shard_map/pallas_call | solution.py:167
  131.7 5.8 %all-to-all-start.1 = ((bf16[32,272,128]{2,1,0:T(8,128)(2,1)}), bf16[32,272,128]{2,1,0:T(8,128)(2,1)S(1)}, u32[]{:S(2)}, u32[]{:S(2)}) async-start(bf16[32,272,128]{2,1,0:T(8,128)(2,1)} %shard_map.103), calls=%async_computation.1 | async-start | bytes 4456448 | tf_op jit(solution)/shard_map/all_to_all | solution.py:535
  137.6 6.1 %shard_map.102 = (f32[16,256,128]{2,1,0:T(8,128)}, f32[16,256,128]{2,1,0:T(8,128)}) custom-call(bf16[16,256,128]{2,1,0:T(8,128)(2,1)} %get-tuple-element.13.q_ref, bf16[128,512]{1,0:T(8,128)(2,1)} %get-tuple-element.14.k_ref, bf16[128,512]{1,0:T(8,128)(2,1)} %get-tuple-element.15.v_ref), custom_call_target="tpu_custom_call" | custom-call | tf_op jit(solution)/shard_map/pallas_call | solution.py:223
  143.7 44.1 %all-to-all-done.1.in_ref = bf16[32,272,128]{2,1,0:T(8,128)(2,1)S(1)} async-done(((bf16[32,272,128]{2,1,0:T(8,128)(2,1)}), bf16[32,272,128]{2,1,0:T(8,128)(2,1)S(1)}, u32[]{:S(2)}, u32[]{:S(2)}) %all-to-all-start.1) | async-done | bytes 2228256 | tf_op jit(solution)/shard_map/all_to_all | solution.py:535
  187.8 0.0 copy-start
  187.8 1.4 copy-done
  189.2 6.1 %shard_map.104 = bf16[128,4096]{1,0:T(8,128)(2,1)} custom-call(s32[32]{0:T(128)} %copy-done.2, f32[16,256,128]{2,1,0:T(8,128)} %get-tuple-element.16.n_ref, f32[16,256,128]{2,1,0:T(8,128)} %get-tuple-element.17.t_ref, bf16[32,272,128]{2,1,0:T(8,128)(2,1)} %copy-done), custom_call_target="tpu_custom_call" | custom-call | tf_op jit(solution)/shard_map/pallas_call | solution.py:256
  (6 shorter events, 0.1 us)
Async XLA Ops:
  2.8 4.5 %copy-start.2 = (s32[32]{0:T(128)}, s32[32]{0:T(128)S(1)}, u32[]{:S(2)}) copy-start(s32[32]{0:T(128)S(1)} %add_bitcast_fusion.at_ref) | copy-start | bytes 388
  7.3 112.0 %all-to-all-start = ((bf16[32,256,128]{2,1,0:T(8,128)(2,1)}), bf16[32,256,128]{2,1,0:T(8,128)(2,1)S(1)}, u32[]{:S(2)}, u32[]{:S(2)}) async-start(bf16[32,256,128]{2,1,0:T(8,128)(2,1)} %get-tuple-element.18), calls=%async_computation | async-start | bytes 4194304 | tf_op jit(solution)/shard_map/all_to_all | solution.py:519
  119.3 1.3 copy-start.1
  131.7 56.1 %all-to-all-start.1 = ((bf16[32,272,128]{2,1,0:T(8,128)(2,1)}), bf16[32,272,128]{2,1,0:T(8,128)(2,1)S(1)}, u32[]{:S(2)}, u32[]{:S(2)}) async-start(bf16[32,272,128]{2,1,0:T(8,128)(2,1)} %shard_map.103), calls=%async_computation.1 | async-start | bytes 4456448 | tf_op jit(solution)/shard_map/all_to_all | solution.py:535
  187.8 1.4 copy-start
